TPU v7x, 32 devices: a whole 2x2x4 slice. The times are simulated.
32 devices in a mesh: tm: 8 (over z, x), head: 4 (over y, core).
Axes of the slice: x: 2, y: 2, z: 4, core: 2. Of those that a mesh axis runs over, the one named last changes fastest.
Arguments:
- frames: float32 [2, 4096, 512], P(None, 'tm'), may hold values from -6 to 6
- cotangent: float32 [2, 4096, 512], P(None, 'tm'), may hold values from -6 to 6
- seg_counts: int32 [2, 4], replicated, may hold values from 1 to 225, as said below
- query_weight: float32 [512, 512], P(None, 'head'), may hold values from -0.25 to 0.25
- query_bias: float32 [512], P('head'), may hold values from -3 to 3
- key_weight: float32 [512, 512], P(None, 'head'), may hold values from -0.25 to 0.25
- value_weight: float32 [512, 512], P(None, 'head'), may hold values from -0.25 to 0.25
- value_bias: float32 [512], P('head'), may hold values from -3 to 3
- out_weight: float32 [512, 512], P('head'), may hold values from -0.75 to 0.75
- out_bias: float32 [512], replicated, may hold values from -3 to 3
- first_gain: float32 [512], replicated, may hold values from 0.25 to 1.75
- first_shift: float32 [512], replicated, may hold values from -2 to 2
- second_gain: float32 [512], replicated, may hold values from 0.25 to 1.75
- second_shift: float32 [512], replicated, may hold values from -2 to 2
- inner_weight: float32 [512, 2048], P(None, 'head'), may hold values from -0.25 to 0.25
- inner_bias: float32 [2048], P('head'), may hold values from -3 to 3
- outer_weight: float32 [2048, 512], P('head'), may hold values from -0.1875 to 0.1875
- outer_bias: float32 [512], replicated, may hold values from -3 to 3
Outputs:
- layer_output: float32 [2, 4096, 512], P(None, 'tm')
- frames_grad: float32 [2, 4096, 512], P(None, 'tm')
- query_weight_grad: float32 [512, 512], P(None, 'head')
- query_bias_grad: float32 [512], P('head')
- key_weight_grad: float32 [512, 512], P(None, 'head')
- value_weight_grad: float32 [512, 512], P(None, 'head')
- value_bias_grad: float32 [512], P('head')
- out_weight_grad: float32 [512, 512], P('head')
- out_bias_grad: float32 [512], replicated
- first_gain_grad: float32 [512], replicated
- first_shift_grad: float32 [512], replicated
- second_gain_grad: float32 [512], replicated
- second_shift_grad: float32 [512], replicated
- inner_weight_grad: float32 [512, 2048], P(None, 'head')
- inner_bias_grad: float32 [2048], P('head')
- outer_weight_grad: float32 [2048, 512], P('head')
- outer_bias_grad: float32 [512], replicated
Inputs may be any that keep to these rules, and one draw needn't show every extreme that they name: `seg_counts`: each row sums to 256; in each row exactly one utterance has 225 segments, the others at least one.
All inputs are finite; a program needn't handle non-finite values.
Results may differ from a plain program's by a relative error of at most 0.0003.
Values sent between devices are 32-bit elements; how exact they have to be, the bound alone decides.
No kernel may reach another device: no remote copies, remote signals or barrier semaphores. Data moves between devices by JAX's collectives and lax.ppermute only.
A program may use at most 128 MiB of HBM per device.

v0:
```python
import jax
import jax.numpy as jnp
from jax import lax
from jax.sharding import PartitionSpec as P

HEAD_DIM = 64
SEG = 16
RC = 4
LC = 30
MEM = 4


EPSILON = 1e-05
HIGHEST = lax.Precision.HIGHEST
MASKED = -1e30


def from_behind(value, axis, by):
    size = lax.axis_size(axis)
    pairs = [(i, i + by) for i in range(size) if 0 <= i + by < size]
    return lax.ppermute(value, axis, pairs)


def product(left, right):
    return jnp.dot(left, right, precision=HIGHEST)


def layer_norm(inputs, gain, shift):
    centred = inputs - jnp.mean(inputs, axis=-1, keepdims=True)
    variance = jnp.mean(centred * centred, axis=-1, keepdims=True)
    return centred * lax.rsqrt(variance + EPSILON) * gain + shift


def segment_owner(counts, first_index, number, segment_total):
    bounds = jnp.cumsum(counts)
    segment_index = first_index + jnp.arange(number, dtype=jnp.int32)
    utterance = jnp.sum((bounds[None, :] <= segment_index[:, None]).astype(jnp.int32), axis=1)
    inside = (segment_index >= 0) & (segment_index < segment_total)
    return jnp.where(inside, utterance, -1)


def attend(queries, extended, memory_rows, owner_ids):
    seg_count = queries.shape[0]
    feature_width = queries.shape[2]
    head_count = feature_width // HEAD_DIM
    key_span = LC + SEG + RC
    block_count = -(-key_span // SEG)
    blocks = extended.reshape(seg_count + block_count - 1, SEG, extended.shape[1])
    window = jnp.concatenate([blocks[i : i + seg_count] for i in range(block_count)], axis=1)[
        :, :key_span
    ]
    memory = jnp.stack([memory_rows[j : j + seg_count] for j in range(MEM)], axis=1)
    keyset = jnp.concatenate([window, memory], axis=1)
    owners = [
        owner_ids[MEM + (j - LC) // SEG : MEM + (j - LC) // SEG + seg_count]
        for j in range(key_span)
    ]
    owners = owners + [owner_ids[j : j + seg_count] for j in range(MEM)]
    visible = jnp.stack(owners, axis=1) == owner_ids[MEM : MEM + seg_count][:, None]
    key_rows = keyset[:, :, :feature_width].reshape(seg_count, key_span + MEM, head_count, HEAD_DIM)
    value_rows = keyset[:, :, feature_width:].reshape(
        seg_count, key_span + MEM, head_count, HEAD_DIM
    )
    query_rows = queries.reshape(seg_count, SEG, head_count, HEAD_DIM)
    scores = jnp.einsum("nqhd,nkhd->nhqk", query_rows, key_rows, precision=HIGHEST) * HEAD_DIM ** (
        -0.5
    )
    scores = jnp.where(visible[:, None, None, :], scores, MASKED)
    scores = scores - jnp.max(scores, axis=-1, keepdims=True)
    weights = jnp.exp(scores)
    weights = weights / jnp.sum(weights, axis=-1, keepdims=True)
    mixture = jnp.einsum("nhqk,nkhd->nqhd", weights, value_rows, precision=HIGHEST)
    return mixture.reshape(seg_count * SEG, feature_width)


def project(normed, query_weight, query_bias, key_weight, value_weight, value_bias):
    queries = product(normed, query_weight) + query_bias
    keyvals = jnp.concatenate(
        [product(normed, key_weight), product(normed, value_weight) + value_bias], axis=1
    )
    summary = jnp.mean(keyvals.reshape(-1, SEG, keyvals.shape[1]), axis=1)
    return (queries, keyvals, summary)


def feed(normed, inner_weight, inner_bias, outer_weight):
    return product(
        jax.nn.gelu(product(normed, inner_weight) + inner_bias, approximate=False), outer_weight
    )


def per_device(
    frames,
    cotangent,
    seg_counts,
    query_weight,
    query_bias,
    key_weight,
    value_weight,
    value_bias,
    out_weight,
    out_bias,
    first_gain,
    first_shift,
    second_gain,
    second_shift,
    inner_weight,
    inner_bias,
    outer_weight,
    outer_bias,
):
    micro_count = frames.shape[0]
    length = frames.shape[1]
    seg_count = length // SEG
    feature_width = query_weight.shape[1]
    seg_total = seg_count * lax.axis_size("tm")
    first_index = lax.axis_index("tm") * seg_count - MEM
    key_span = LC + SEG + RC
    block_count = -(-key_span // SEG)
    padding = (seg_count + block_count - 1) * SEG - (LC + length + RC)
    params = (
        query_weight,
        query_bias,
        key_weight,
        value_weight,
        value_bias,
        out_weight,
        out_bias,
        first_gain,
        first_shift,
        second_gain,
        second_shift,
        inner_weight,
        inner_bias,
        outer_weight,
        outer_bias,
    )
    totals = tuple((jnp.zeros_like(p) for p in params))
    results = []
    input_grads = []
    for batch_index in range(micro_count):
        owner_ids = segment_owner(
            seg_counts[batch_index], first_index, seg_count + MEM + 2, seg_total
        )
        inputs = frames[batch_index]
        normed, first_pull = jax.vjp(layer_norm, inputs, first_gain, first_shift)
        (queries, keyvals, summary), project_pull = jax.vjp(
            project, normed, query_weight, query_bias, key_weight, value_weight, value_bias
        )
        kv_width = keyvals.shape[1]
        cache_pack = jnp.concatenate([keyvals[length - LC :], summary[seg_count - MEM :]], axis=0)
        cache_recv = from_behind(cache_pack, "tm", 1)
        ahead_recv = from_behind(keyvals[:RC], "tm", -1)

        def local_attend(query_in, keyval_in, summary_in, cache_in, ahead_in):
            extended = jnp.concatenate(
                [cache_in[:LC], keyval_in, ahead_in, jnp.zeros((padding, kv_width), jnp.float32)],
                axis=0,
            )
            memory_rows = jnp.concatenate([cache_in[LC:], summary_in], axis=0)
            return attend(
                query_in.reshape(seg_count, SEG, feature_width), extended, memory_rows, owner_ids
            )

        mixture, attend_pull = jax.vjp(
            local_attend, queries, keyvals, summary, cache_recv, ahead_recv
        )
        mixed_total = lax.psum(product(mixture, out_weight), "head")
        middle = inputs + mixed_total + out_bias
        normed_two, second_pull = jax.vjp(layer_norm, middle, second_gain, second_shift)
        inner_part, feed_pull = jax.vjp(feed, normed_two, inner_weight, inner_bias, outer_weight)
        inner_total = lax.psum(inner_part, "head")
        results.append(middle + inner_total + outer_bias)
        upstream = cotangent[batch_index]
        outer_bias_step = jnp.sum(upstream, axis=0)
        normed_two_part, inner_weight_step, inner_bias_step, outer_weight_step = feed_pull(upstream)
        normed_two_grad = lax.psum(normed_two_part, "head")
        middle_norm_grad, second_gain_step, second_shift_step = second_pull(normed_two_grad)
        middle_grad = upstream + middle_norm_grad
        out_bias_step = jnp.sum(middle_grad, axis=0)
        out_weight_step = product(mixture.T, middle_grad)
        mixture_grad = product(middle_grad, out_weight.T)
        query_grad, keyval_grad, summary_grad, cache_grad, ahead_grad = attend_pull(mixture_grad)
        cache_return = from_behind(cache_grad, "tm", -1)
        ahead_return = from_behind(ahead_grad, "tm", 1)
        keyval_grad = keyval_grad.at[length - LC :].add(cache_return[:LC]).at[:RC].add(ahead_return)
        summary_grad = summary_grad.at[seg_count - MEM :].add(cache_return[LC:])
        (
            normed_part,
            query_weight_step,
            query_bias_step,
            key_weight_step,
            value_weight_step,
            value_bias_step,
        ) = project_pull((query_grad, keyval_grad, summary_grad))
        normed_grad = lax.psum(normed_part, "head")
        inputs_norm_grad, first_gain_step, first_shift_step = first_pull(normed_grad)
        input_grads.append(middle_grad + inputs_norm_grad)
        steps_now = (
            query_weight_step,
            query_bias_step,
            key_weight_step,
            value_weight_step,
            value_bias_step,
            out_weight_step,
            out_bias_step,
            first_gain_step,
            first_shift_step,
            second_gain_step,
            second_shift_step,
            inner_weight_step,
            inner_bias_step,
            outer_weight_step,
            outer_bias_step,
        )
        steps_now = lax.psum(
            (
                steps_now[0],
                steps_now[1],
                steps_now[2],
                steps_now[3],
                steps_now[4],
                steps_now[5],
                steps_now[6],
                steps_now[7],
                steps_now[8],
                steps_now[9],
                steps_now[10],
                steps_now[11],
                steps_now[12],
                steps_now[13],
                steps_now[14],
            ),
            "tm",
        )
        totals = tuple((t + s for t, s in zip(totals, steps_now)))
    return (jnp.stack(results), jnp.stack(input_grads)) + tuple(totals)


def solution(mesh):
    in_specs = (
        P(None, "tm", None),
        P(None, "tm", None),
        P(),
        P(None, "head"),
        P("head"),
        P(None, "head"),
        P(None, "head"),
        P("head"),
        P("head", None),
        P(),
        P(),
        P(),
        P(),
        P(),
        P(None, "head"),
        P("head"),
        P("head", None),
        P(),
    )
    out_specs = (
        P(None, "tm", None),
        P(None, "tm", None),
        P(None, "head"),
        P("head"),
        P(None, "head"),
        P(None, "head"),
        P("head"),
        P("head", None),
        P(),
        P(),
        P(),
        P(),
        P(),
        P(None, "head"),
        P("head"),
        P("head", None),
        P(),
    )
    return jax.shard_map(
        per_device, mesh=mesh, in_specs=in_specs, out_specs=out_specs, check_vma=False
    )
```

profile of v0, /device:TPU:0, one launch (start us, length us, event | category | flops | bytes accessed | tf_op | source)
XLA Modules:
  0.0 679.0 jit_solution(6140783813603447381)
XLA Ops:
  51.7 6.9 %collective-permute-start = (f32[34,256]{0,1:T(8,128)}, f32[34,256]{0,1:T(8,128)}, u32[]{:S(2)}, u32[]{:S(2)}) collective-permute-start(f32[34,256]{0,1:T(8,128)} %pad_maximum_fusion.18), channel_id=1, source_target_pairs={{0,4},{4,8},{8,12},{12,16},{16,20},{20,24},{24,28},{1,5},{5,9},{9,... | collective-permute-start | bytes 104456 | tf_op jit(solution)/shard_map/ppermute | solution.py:21
  77.2 4.4 collective-permute-start.2
  99.7 6.9 %concatenate.79 = f32[32,54,256]{2,1,0:T(8,128)} concatenate(f32[32,50,256]{2,1,0:T(8,128)} %pad_maximum_fusion.5, f32[32,1,256]{2,1,0:T(1,128)} %stack.56, f32[32,1,256]{2,1,0:T(1,128)} %stack.57, f32[32,1,256]{2,1,0:T(1,128)} %stack.58, f32[32,1,256]{2,1,0:T(1,128)} %stack.59), dimensions={1} | concatenate | bytes 3538944 | tf_op jit(solution)/shard_map/jvp()/concatenate | solution.py:53
  125.3 6.9 %concatenate.87 = f32[32,54,256]{2,1,0:T(8,128)} concatenate(f32[32,50,256]{2,1,0:T(8,128)} %pad_maximum_fusion.2, f32[32,1,256]{2,1,0:T(1,128)S(1)} %stack.68, f32[32,1,256]{2,1,0:T(1,128)S(1)} %stack.69, f32[32,1,256]{2,1,0:T(1,128)S(1)} %stack.70, f32[32,1,256]{2,1,0:T(1,128)S(1)} %stack.71), dimensions={1} | concatenate | bytes 3538944 | tf_op jit(solution)/shard_map/jvp()/concatenate | solution.py:53
  141.3 4.8 fusion.237
  151.6 3.6 reshape.1451
  155.2 4.8 fusion.238
  172.8 51.6 %all-reduce.40.cloned.1.call-done = (f32[512,512]{1,0:T(8,128)}, f32[512,512]{1,0:T(8,128)}) async-done(((f32[512,512]{1,0:T(8,128)}, f32[512,512]{1,0:T(8,128)}), (f32[512,512]{1,0:T(8,128)}, f32[512,512]{1,0:T(8,128)})) %all-reduce.40.cloned.1.call-update) | async-done | bytes 2097168 | tf_op jit(solution)/shard_map/psum | solution.py:167
  226.6 4.1 fusion.42
  242.8 4.1 fusion.43
  267.1 38.2 %all-reduce.38.cloned.1.call-done = (f32[512,512]{1,0:T(8,128)}, f32[512,512]{1,0:T(8,128)}) async-done(((f32[512,512]{1,0:T(8,128)}, f32[512,512]{1,0:T(8,128)}), (f32[512,512]{1,0:T(8,128)}, f32[512,512]{1,0:T(8,128)})) %all-reduce.38.cloned.1.call-update) | async-done | bytes 2097168 | tf_op jit(solution)/shard_map/psum | solution.py:176
  317.0 6.4 convert_reduce_fusion.1
  327.9 4.9 convert_reduce_fusion
  337.6 3.4 convolution_bitcast_fusion
  344.3 4.6 convolution_bitcast_fusion.2
  348.9 5.1 convolution_bitcast_fusion.1
  359.3 3.7 copy.401
  368.3 4.7 convolution_bitcast_fusion.3
  378.3 3.6 copy.393
  404.6 5.1 collective-permute-start.5
  409.7 4.3 collective-permute-start.7
  462.5 63.2 %all-reduce.36.cloned.1.call-done = (f32[512,512]{1,0:T(8,128)}, f32[512,512]{1,0:T(8,128)}, f32[512,512]{1,0:T(8,128)}, f32[512,512]{1,0:T(8,128)}) async-done(((f32[512,512]{1,0:T(8,128)}, f32[512,512]{1,0:T(8,128)}, f32[512,512]{1,0:T(8,128)}, f32[512,512]{1,0:T(8,128)}), (f32[512,512]{1,0:T(8,128)}, f32[512,512]{1,0:T(8,128)}, f32[512,512]{1,0:T(8,128)}, ...) | async-done | bytes 4194320 | tf_op jit(solution)/shard_map/psum | solution.py:171
  528.1 39.5 %all-reduce.24 = (f32[128]{0:T(128)}, f32[128]{0:T(128)}, f32[512]{0:T(512)}, f32[512]{0:T(512)}, f32[512]{0:T(512)}, /*index=5*/f32[512]{0:T(512)}, f32[512]{0:T(512)}, f32[512]{0:T(512)}, f32[512]{0:T(512)}) all-reduce(f32[128]{0:T(128)S(1)} %reshape.1450, f32[128]{0:T(128)S(1)} %add.448, ...), channel_id=1, replica_groups=mesh['tm'=8,'head'=4] {'tm'}, use_global_device_ids=true, to_apply=%region_43.44 | all-reduce | flops 3840 | bytes 30720 | tf_op jit(solution)/shard_map/psum | solution.py:215
  576.3 86.7 %all-reduce.34.cloned.1.call-done = (f32[512,128]{1,0:T(8,128)}, f32[512,128]{1,0:T(8,128)}, f32[512,128]{1,0:T(8,128)}, f32[128,512]{1,0:T(8,128)}, f32[512,512]{1,0:T(8,128)}, /*index=5*/f32[512,512]{1,0:T(8,128)}) async-done(((f32[512,128]{1,0:T(8,128)}, f32[512,128]{1,0:T(8,128)}, f32[512,128]{1,0:T(8,128)}, f32[128,512]{1,0:T(8,128)}, f32[512,512]{1,0:T(8,128)}, /*index=5*/f32[512,512]{1,0:T(8,128)}), ...) | async-done | bytes 3145744 | tf_op jit(solution)/shard_map/psum | solution.py:215
  (496 shorter events, 291.3 us)
Async XLA Ops:
  7.2 219.4 %copy-start = (f32[512,512]{1,0:T(8,128)S(1)}, f32[512,512]{1,0:T(8,128)}, u32[]{:S(2)}) copy-start(f32[512,512]{1,0:T(8,128)} %param.44) | copy-start | bytes 3145732
  7.2 217.2 %all-reduce.40.cloned.1.call-start = ((), (), s32[]{:S(2)}) async-start(), calls=%async_computation.3 | async-start | bytes 4194304 | tf_op jit(solution)/shard_map/psum | solution.py:167
  10.0 11.4 %copy-start.88 = (f32[512]{0:T(512)}, f32[512]{0:T(512)S(1)}, u32[]{:S(2)}) copy-start(f32[512]{0:T(512)S(1)} %fusion.203) | copy-start | bytes 6148
  13.6 45.0 %collective-permute-start.3 = (f32[4,256]{0,1:T(8,128)}, f32[4,256]{0,1:T(8,128)}, u32[]{:S(2)}, u32[]{:S(2)}) collective-permute-start(f32[4,256]{0,1:T(8,128)} %fusion.168), channel_id=1, source_target_pairs={{4,0},{8,4},{12,8},{16,12},{20,16},{24,20},{28,24},{5,1},{9,5},{13... | collective-permute-start | bytes 12296 | tf_op jit(solution)/shard_map/ppermute | solution.py:21
  14.9 8.3 %copy-start.90 = (f32[512]{0:T(512)}, f32[512]{0:T(512)S(1)}, u32[]{:S(2)}) copy-start(f32[512]{0:T(512)S(1)} %fusion.201) | copy-start | bytes 6148
  18.6 22.3 %collective-permute-start.1 = (f32[4,256]{0,1:T(8,128)}, f32[4,256]{0,1:T(8,128)}, u32[]{:S(2)}, u32[]{:S(2)}) collective-permute-start(f32[4,256]{0,1:T(8,128)} %fusion.170), channel_id=1, source_target_pairs={{4,0},{8,4},{12,8},{16,12},{20,16},{24,20},{28,24},{5,1},{9,5},{13... | collective-permute-start | bytes 12296 | tf_op jit(solution)/shard_map/ppermute | solution.py:21
  40.9 9.1 %copy-start.70 = (f32[30,256]{0,1:T(8,128)S(1)}, f32[30,256]{0,1:T(8,128)}, u32[]{:S(2)}) copy-start(f32[30,256]{0,1:T(8,128)} %fusion.169) | copy-start | bytes 92164
  51.7 15.6 %copy-start.69 = (f32[30,256]{0,1:T(8,128)S(1)}, f32[30,256]{0,1:T(8,128)}, u32[]{:S(2)}) copy-start(f32[30,256]{0,1:T(8,128)} %fusion.167) | copy-start | bytes 92164
  51.7 29.8 %collective-permute-start = (f32[34,256]{0,1:T(8,128)}, f32[34,256]{0,1:T(8,128)}, u32[]{:S(2)}, u32[]{:S(2)}) collective-permute-start(f32[34,256]{0,1:T(8,128)} %pad_maximum_fusion.18), channel_id=1, source_target_pairs={{0,4},{4,8},{8,12},{12,16},{16,20},{20,24},{24,28},{1,5},{5,9},{9,... | collective-permute-start | bytes 104456 | tf_op jit(solution)/shard_map/ppermute | solution.py:21
  77.2 35.6 %collective-permute-start.2 = (f32[34,256]{0,1:T(8,128)}, f32[34,256]{0,1:T(8,128)S(1)}, u32[]{:S(2)}, u32[]{:S(2)}) collective-permute-start(f32[34,256]{0,1:T(8,128)} %pad_maximum_fusion.19), channel_id=1, source_target_pairs={{0,4},{4,8},{8,12},{12,16},{16,20},{20,24},{24,28},{1,5},{5,9},{9,... | collective-permute-start | bytes 104456 | tf_op jit(solution)/shard_map/ppermute | solution.py:21
  146.6 25.5 %copy-start.86 = (f32[32,2,16]{2,1,0:T(2,128)}, f32[32,2,16]{2,1,0:T(2,128)S(1)}, u32[]{:S(2)}) copy-start(f32[32,2,16]{2,1,0:T(2,128)S(1)} %fusion.138) | copy-start | bytes 12292
  160.5 11.0 %copy-start.84 = (f32[32,2,16]{2,1,0:T(2,128)}, f32[32,2,16]{2,1,0:T(2,128)S(1)}, u32[]{:S(2)}) copy-start(f32[32,2,16]{2,1,0:T(2,128)S(1)} %fusion.136) | copy-start | bytes 12292
  168.4 56.0 %copy-start.117 = (f32[512]{0:T(512)S(1)}, f32[512]{0:T(512)}, u32[]{:S(2)}) copy-start(f32[512]{0:T(512)} %param.39) | copy-start | bytes 6148
  171.3 134.0 %all-reduce.38.cloned.1.call-start = ((), (), s32[]{:S(2)}) async-start(), calls=%async_computation.2 | async-start | bytes 4194304 | tf_op jit(solution)/shard_map/psum | solution.py:176
  226.3 16.5 %copy-start.5 = (f32[512,512]{1,0:T(8,128)}, f32[512,512]{1,0:T(8,128)S(1)}, u32[]{:S(2)}) copy-start(f32[512,512]{1,0:T(8,128)S(1)} %get-tuple-element.161) | copy-start | bytes 3145732
  253.5 272.2 %all-reduce.36.cloned.1.call-start = ((), (), s32[]{:S(2)}) async-start(), calls=%async_computation.1 | async-start | bytes 8388608 | tf_op jit(solution)/shard_map/psum | solution.py:171
  317.0 7.0 %copy-start.13 = (f32[512,512]{1,0:T(8,128)S(1)}, f32[512,512]{1,0:T(8,128)}, u32[]{:S(2)}) copy-start(f32[512,512]{1,0:T(8,128)} %get-tuple-element.163) | copy-start | bytes 3145732
  390.3 25.0 %collective-permute-start.6 = (f32[34,256]{1,0:T(8,128)}, f32[34,256]{1,0:T(8,128)}, u32[]{:S(2)}, u32[]{:S(2)}) collective-permute-start(f32[34,256]{1,0:T(8,128)} %get-tuple-element.212), channel_id=1, source_target_pairs={{4,0},{8,4},{12,8},{16,12},{20,16},{24,20},{28,24},{5,1},{9,5},{13... | collective-permute-start | bytes 104456 | tf_op jit(solution)/shard_map/ppermute | solution.py:21
  400.4 23.6 %copy-start.53 = (f32[512,128]{1,0:T(8,128)S(1)}, f32[512,128]{1,0:T(8,128)}, u32[]{:S(2)}) copy-start(f32[512,128]{1,0:T(8,128)} %param.36) | copy-start | bytes 786436
  404.6 24.9 %collective-permute-start.5 = (f32[4,256]{1,0:T(4,128)}, f32[4,256]{1,0:T(4,128)}, u32[]{:S(2)}, u32[]{:S(2)}) collective-permute-start(f32[4,256]{1,0:T(4,128)} %split.101), channel_id=1, source_target_pairs={{0,4},{4,8},{8,12},{12,16},{16,20},{20,24},{24,28},{1,5},{5,9},{9,... | collective-permute-start | bytes 12296 | tf_op jit(solution)/shard_map/ppermute | solution.py:21
  409.7 9.8 %collective-permute-start.7 = (f32[4,256]{1,0:T(4,128)}, f32[4,256]{1,0:T(4,128)}, u32[]{:S(2)}, u32[]{:S(2)}) collective-permute-start(f32[4,256]{1,0:T(4,128)} %split.114), channel_id=1, source_target_pairs={{0,4},{4,8},{8,12},{12,16},{16,20},{20,24},{24,28},{1,5},{5,9},{9,... | collective-permute-start | bytes 12296 | tf_op jit(solution)/shard_map/ppermute | solution.py:21
  414.0 12.0 %collective-permute-start.4 = (f32[34,256]{1,0:T(8,128)}, f32[34,256]{1,0:T(8,128)}, u32[]{:S(2)}, u32[]{:S(2)}) collective-permute-start(f32[34,256]{1,0:T(8,128)} %get-tuple-element.211), channel_id=1, source_target_pairs={{4,0},{8,4},{12,8},{16,12},{20,16},{24,20},{28,24},{5,1},{9,5},{13... | collective-permute-start | bytes 104456 | tf_op jit(solution)/shard_map/ppermute | solution.py:21
  439.2 223.9 %all-reduce.34.cloned.1.call-start = ((), (), s32[]{:S(2)}) async-start(), calls=%async_computation | async-start | bytes 6291456 | tf_op jit(solution)/shard_map/psum | solution.py:215
  525.8 41.9 %copy-start.118 = (f32[512]{0:T(512)S(1)}, f32[512]{0:T(512)}, u32[]{:S(2)}) copy-start(f32[512]{0:T(512)} %param.47) | copy-start | bytes 6148
  (112 other events, 349.0 us)
Sparse Core Ops, SparseCore 0:
  171.4 52.9 all-reduce.39
  253.6 51.6 all-reduce.37
  439.3 86.4 all-reduce.35
  531.1 131.9 all-reduce.33
where the time goes:
time: 691 us; the launch traced here: 679 us
  waiting for transfers between devices  240 us (35%)
  local copies, waits for them, and re-layouts  150 us (22%)
  matrix products  135 us (20%)
  other arithmetic  71.9 us (10%)
  blocking collectives  39.5 us (6%)
  starting transfers between devices  26.8 us (4%)
  between operations  16 us (2%)
    psum x1, waiting for transfers between devices, per_device(): lax.psum((steps_now[0], steps_now[1], steps_now[2], steps_now[3], steps_n...  86.7 us
    dot_general x36, matrix products, product(): return jnp.dot(left, right, precision=HIGHEST)  86.3 us
    psum x1, waiting for transfers between devices, per_device(): inner_total = lax.psum(inner_part, 'head')  63.2 us
    psum x1, waiting for transfers between devices, per_device(): mixed_total = lax.psum(product(mixture, out_weight), 'head')  51.6 us
    psum x1, blocking collectives, per_device(): lax.psum((steps_now[0], steps_now[1], steps_now[2], steps_now[3], steps_n...  39.5 us
    psum x1, waiting for transfers between devices, per_device(): normed_two_grad = lax.psum(normed_two_part, 'head')  38.2 us
    ppermute x8, starting transfers between devices, from_behind(): return lax.ppermute(value, axis, pairs)  25.8 us
    dot_general x6, matrix products, attend(): jnp.einsum('nhqk,nkhd->nqhd', weights, value_rows, precision=HIGHEST)  24.8 us
  transfers between devices with their start and end apart: 12, of which 4 were waited for; matrix products, arithmetic and copies ran while one was open for 23% of the time, Pallas kernels for 0%

commit v1 on v0

v1 whole, which is shorter than its diff:
```python
import functools

import jax
import jax.numpy as jnp
from jax import lax
from jax.experimental import pallas as pl
from jax.experimental.pallas import tpu as pltpu
from jax.sharding import PartitionSpec as P

HEAD_DIM = 64
SEG = 16
RC = 4
LC = 30
MEM = 4

EPSILON = 1e-05
MASKED = -1e30
F32 = jnp.float32

CACHE = 32
SUMS = 8
AHEAD = 8
BLOCK = 64
WIN = CACHE + BLOCK + AHEAD
SWIN = 16
KEYS = 128
FIRST_GAIN, SECOND_GAIN, SECOND_SHIFT, OUT_BIAS, INNER_BIAS, OUTER_BIAS = range(6)
PAIR = 2 * HEAD_DIM
MIB = 1 << 20


def mm(left, right, left_dim=1, right_dim=0):
    return lax.dot_general(
        left,
        right,
        (((left_dim,), (right_dim,)), ((), ())),
        precision=lax.Precision.HIGH,
        preferred_element_type=F32,
    )


def normalise(values):
    centred = values - jnp.mean(values, axis=-1, keepdims=True)
    variance = jnp.mean(centred * centred, axis=-1, keepdims=True)
    rate = lax.rsqrt(variance + EPSILON)
    return centred * rate, rate


def norm_back(grad, gain, xhat, rate):
    scaled = grad * gain
    first = jnp.mean(scaled, axis=-1, keepdims=True)
    second = jnp.mean(scaled * xhat, axis=-1, keepdims=True)
    return rate * (scaled - first - xhat * second)


def column_sums(values):
    return jnp.sum(values, axis=0, keepdims=True)


def seg_means(values):
    rows, width = values.shape
    return jnp.sum(values.reshape(rows // SEG, SEG, width), axis=1) * (1.0 / SEG)


def near_bit():
    return lax.axis_index("head") % 2


def far_bit():
    return lax.axis_index("head") // 2


def my_rows(rows):
    half = rows // 2
    return pl.ds(pl.multiple_of(near_bit() * half, half), half)


def lanes_of(place, width, start=0):
    at = place + near_bit() - 2 * place * near_bit()
    return pl.ds(pl.multiple_of(start + at * width, width), width)


def full(shape):
    return pl.BlockSpec(shape, lambda *_: (0,) * len(shape))


def micro_block(shape, index):
    return pl.BlockSpec((1,) + shape, lambda *_: (index,) + (0,) * len(shape))


class Steps:
    def __init__(self):
        self.held = []

    def hold(self, *values):
        self.held.extend(values)

    def call(self, kernel, name, us, outs, args, specs=None, scratch=(), vmem=32, copies=0, far=(), far_outs=()):
        specs = dict(specs or {})
        given, made, held = len(args), len(outs), tuple(self.held)
        token = bool(far_outs)
        somewhere = pl.BlockSpec(memory_space=pl.ANY)
        in_hbm = pl.BlockSpec(memory_space=pltpu.HBM)

        def body(*refs):
            ins, rest = refs[:given], refs[given + len(held) :]
            if token:
                rest[made][...] = jnp.zeros(rest[made].shape, F32)
            kernel(*ins, *rest[:made], *rest[made + token :])

        args = [pltpu.with_memory_space_constraint(a, pltpu.HBM) if i in far else a for i, a in enumerate(args)]
        out_specs = [in_hbm if i in far_outs else full(shape) for i, shape in enumerate(outs)]
        out_shape = [
            pltpu.HBM(shape, F32) if i in far_outs else jax.ShapeDtypeStruct(shape, F32) for i, shape in enumerate(outs)
        ]
        if token:
            out_specs.append(full((1, 128)))
            out_shape.append(jax.ShapeDtypeStruct((1, 128), F32))
        out = pl.pallas_call(
            body,
            name=name,
            grid=(1,),
            in_specs=[in_hbm if i in far else specs.get(i, full(a.shape)) for i, a in enumerate(args)]
            + [somewhere] * len(held),
            out_specs=out_specs,
            out_shape=out_shape,
            scratch_shapes=[pltpu.VMEM(shape, F32) for shape in scratch]
            + ([pltpu.SemaphoreType.DMA((copies,))] if copies else []),
            compiler_params=pltpu.CompilerParams(vmem_limit_bytes=vmem * MIB),
            cost_estimate=pl.CostEstimate(flops=int(us * 5.18e8), bytes_accessed=0, transcendentals=0),
        )(*args, *held)
        self.held = [out[-1]]
        return out[:made]


def copy_all(pairs, sems):
    copies = [pltpu.make_async_copy(a, b, sems.at[i]) for i, (a, b) in enumerate(pairs)]
    for copy in copies:
        copy.start()
    return copies


def norm_kernel(frames, gain, shift, wq, wk, wv, bq, bv, x_ref, xhat_ref, rate_ref, normed_ref, w_ref, b_ref, params, sems):
    micros, half, _ = x_ref.shape
    rows = frames.shape[1]
    width = wq.shape[1]
    pairs = [(gain, params.at[pl.ds(0, 1)]), (shift, params.at[pl.ds(8, 1)])]
    pairs += [(frames.at[m, my_rows(rows)], x_ref.at[m]) for m in range(micros)]
    pairs += [(w, w_ref.at[:, pl.ds(i * width, width)]) for i, w in enumerate((wq, wk, wv))]
    pairs += [(b, b_ref.at[:, pl.ds(i * width, width)]) for i, b in enumerate((bq, bv))]
    copies = copy_all(pairs, sems)
    for copy in copies[:2]:
        copy.wait()
    for micro in range(micros):
        copies[2 + micro].wait()
        xhat, rate = normalise(x_ref[micro])
        xhat_ref[micro] = xhat
        rate_ref[micro] = jnp.broadcast_to(rate, (half, rate_ref.shape[2]))
        normed_ref[micro] = xhat * params[0:1] + params[8:9]
    for copy in copies[micros + 2 :]:
        copy.wait()


def project_kernel(
    normed, own, b_own, q_pair, k_pair, v_pair, bq_pair, bv_pair, wi, wu, wo, cotangent, g1, g2, s2, bo, bi, bu,
    q_ref, kv_ref, tail_ref, head_ref, w_ref, wi_ref, wu_ref, wo_ref, g_ref, rows_ref,
    bias, sems,
):
    micros, half, _ = normed.shape
    width = q_pair.shape[1]
    pairs = [(wi, wi_ref), (wu, wu_ref), (wo, wo_ref)]
    pairs += [(cotangent.at[m, my_rows(cotangent.shape[1])], g_ref.at[m]) for m in range(micros)]
    pairs += [(v, rows_ref.at[i]) for i, v in enumerate((g1, g2, s2, bo, bi, bu))]
    copies = copy_all(pairs, sems)
    for number, pair in enumerate((q_pair, k_pair, v_pair)):
        at = 2 * number * width
        w_ref[:, lanes_of(0, width, at)] = own[:, number * width : (number + 1) * width]
        w_ref[:, lanes_of(1, width, at)] = pair[...]
    bias[...] = jnp.zeros_like(bias)
    bias[:, lanes_of(0, width)] = b_own[:, :width]
    bias[:, lanes_of(1, width)] = bq_pair[...]
    bias[:, lanes_of(0, width, 4 * width)] = b_own[:, width:]
    bias[:, lanes_of(1, width, 4 * width)] = bv_pair[...]
    for micro in range(micros):
        out = mm(normed[micro], w_ref[...]) + bias[...]
        q_ref[micro] = out[:, : 2 * width]
        kv_ref[micro] = out[:, 2 * width :]
        tail_ref[micro, :CACHE] = kv_ref[micro, half - CACHE :]
        tail_ref[micro, CACHE:] = seg_means(kv_ref[micro, half - SUMS * SEG :])
        head_ref[micro] = kv_ref[micro, :AHEAD]
    for copy in copies:
        copy.wait()


def fill_keys(kv, cache, ahead, kx, sx):
    length = kv.shape[0]
    segs = length // SEG
    kx[CACHE : CACHE + length] = kv
    sx[SUMS : SUMS + segs] = seg_means(kv)
    if cache is not None:
        kx[:CACHE] = cache[:CACHE]
        kx[CACHE + length :] = ahead
        sx[:SUMS] = cache[CACHE:]
        sx[SUMS + segs :] = jnp.zeros((SUMS, kv.shape[1]), F32)


def summary_start(block):
    return (block * (BLOCK // SEG) + SUMS - MEM) // SUMS * SUMS


def key_window(kx, sx, block, lanes):
    start = summary_start(block)
    rows = [kx[block * BLOCK : block * BLOCK + WIN, lanes], sx[start : start + SWIN, lanes]]
    return jnp.concatenate(rows + [jnp.zeros((KEYS - WIN - SWIN, PAIR), F32)], axis=0)


def by_head(values):
    first = lax.broadcasted_iota(jnp.int32, values.shape, 1) < HEAD_DIM
    return jnp.concatenate([jnp.where(first, values, 0.0), jnp.where(first, 0.0, values)], axis=0)


def side_by_side(values):
    rows = values.shape[0] // 2
    first = lax.broadcasted_iota(jnp.int32, (rows, values.shape[1]), 1) < HEAD_DIM
    return jnp.where(first, values[:rows], values[rows:])


def owner_of(segment, bounds):
    owner = jnp.where(segment < 0, -1, 0)
    for bound in bounds:
        owner = owner + (segment >= bound).astype(jnp.int32)
    return owner


def visible(block, base, bounds):
    row = lax.broadcasted_iota(jnp.int32, (2 * BLOCK, 1), 0) % BLOCK
    column = lax.broadcasted_iota(jnp.int32, (1, KEYS), 1)
    query_seg = block * (BLOCK // SEG) + row // SEG
    frame = block * BLOCK - CACHE + column
    is_frame = column < WIN
    summary = summary_start(block) - SUMS + column - WIN
    key_seg = jnp.where(is_frame, (frame + CACHE) // SEG - CACHE // SEG, summary)
    key_seg = jnp.where(column < WIN + SWIN, key_seg, -(1 << 20))
    inside = (frame >= query_seg * SEG - LC) & (frame < query_seg * SEG + SEG + RC)
    near = (key_seg >= query_seg - MEM) & (key_seg < query_seg)
    seen = (is_frame & inside) | ((column >= WIN) & near)
    return seen & (owner_of(key_seg + base, bounds) == owner_of(query_seg + base, bounds))


def bounds_of(counts, micro):
    bounds, total = [], 0
    for utterance in range(counts.shape[1]):
        total = total + counts[micro, utterance]
        bounds.append(total)
    return bounds


def first_segment(length):
    return (lax.axis_index("tm") * 2 + near_bit()) * (length // SEG)


def attend_block(block, seen, query, kx, sx, keep, put):
    width = query.shape[1]
    for pair in range(width // PAIR):
        lanes = slice(pair * PAIR, (pair + 1) * PAIR)
        value_lanes = slice(width + pair * PAIR, width + (pair + 1) * PAIR)
        scores = mm(by_head(query[:, lanes] * HEAD_DIM ** (-0.5)), key_window(kx, sx, block, lanes), 1, 1)
        scores = jnp.where(seen, scores, MASKED)
        weights = jnp.exp(scores - jnp.max(scores, axis=-1, keepdims=True))
        weights = weights / jnp.sum(weights, axis=-1, keepdims=True)
        keep(pair, weights)
        put(lanes, side_by_side(mm(weights, key_window(kx, sx, block, value_lanes))))


def block_rows(block):
    return slice(block * BLOCK, (block + 1) * BLOCK)


def attend_inner_kernel(counts, q_ref, kv_ref, mix_ref, p_ref, kx, sx):
    micros, length, _ = q_ref.shape
    blocks = length // BLOCK
    base = first_segment(length)
    for micro in range(micros):
        fill_keys(kv_ref[micro], None, None, kx, sx)
        bounds = bounds_of(counts, micro)
        for number, block in enumerate(range(1, blocks - 1)):
            def keep(pair, weights):
                p_ref[micro, number, pair] = weights

            def put(lanes, values):
                mix_ref[micro, block_rows(number), lanes] = values

            seen = visible(block, base, bounds)
            attend_block(block, seen, q_ref[micro, block_rows(block)], kx, sx, keep, put)


def attend_outer_kernel(micro, counts, q_ref, kv_ref, cache, ahead, inner, *refs):
    *refs, kx, sx = refs
    passed = len(refs) // 2 - 1
    mix_ref, p_ref = refs[passed : passed + 2]
    for source, target in zip(refs[:passed], refs[passed + 2 :], strict=True):
        target[...] = source[...]
    _, length, _ = q_ref.shape
    blocks = length // BLOCK
    base = first_segment(length)
    fill_keys(kv_ref[0], cache[0], ahead[0], kx, sx)
    bounds = bounds_of(counts, micro)
    mix_ref[BLOCK : length - BLOCK] = inner[0]
    for number, block in enumerate((0, blocks - 1)):
        def keep(pair, weights):
            p_ref[number, pair] = weights

        def put(lanes, values):
            mix_ref[block_rows(block), lanes] = values

        seen = visible(block, base, bounds)
        attend_block(block, seen, q_ref[0, block_rows(block)], kx, sx, keep, put)


def back_block(block, weights_of, query, grads, kx, sx, dq_ref, dkx, dsx):
    width = query.shape[1]
    start = summary_start(block)
    frames = slice(block * BLOCK, block * BLOCK + WIN)
    for pair in range(width // PAIR):
        lanes = slice(pair * PAIR, (pair + 1) * PAIR)
        value_lanes = slice(width + pair * PAIR, width + (pair + 1) * PAIR)
        weights = weights_of(pair)
        grad = by_head(grads[:, lanes])
        dweights = mm(grad, key_window(kx, sx, block, value_lanes), 1, 1)
        dscores = weights * (dweights - jnp.sum(dweights * weights, axis=-1, keepdims=True))
        dquery = side_by_side(mm(dscores, key_window(kx, sx, block, lanes)))
        dq_ref[block_rows(block), lanes] = dquery * HEAD_DIM ** (-0.5)
        dkeys = mm(dscores, by_head(query[:, lanes] * HEAD_DIM ** (-0.5)), 0, 0)
        dvalues = mm(weights, grad, 0, 0)
        dkx[frames, lanes] += dkeys[:WIN]
        dkx[frames, value_lanes] += dvalues[:WIN]
        dsx[start : start + SWIN, lanes] += dkeys[WIN : WIN + SWIN]
        dsx[start : start + SWIN, value_lanes] += dvalues[WIN : WIN + SWIN]


def back_outer_kernel(
    a_ref, b_ref, mid_ref, g_ref, params, wo_own, wo_pair, q_ref, kv_ref, cache, ahead, p_ref,
    dmid_ref, dmix_ref, dq_ref, back_ref, fore_ref, vec_ref, dkx, dsx,
    kx, sx,
):
    length, features = mid_ref.shape
    width = wo_own.shape[0]
    blocks = length // BLOCK
    grad = a_ref[...] + b_ref[...]
    xhat, rate = normalise(mid_ref[...])
    dmid = g_ref[0] + norm_back(grad, params[SECOND_GAIN], xhat, rate)
    dmid_ref[...] = dmid
    vec_ref[0:1] = column_sums(dmid)
    vec_ref[1:2] = column_sums(grad * xhat)
    vec_ref[2:3] = column_sums(grad)
    dmix_ref[:, lanes_of(0, width)] = mm(dmid, wo_own[...], 1, 1)
    dmix_ref[:, lanes_of(1, width)] = mm(dmid, wo_pair[...], 1, 1)
    fill_keys(kv_ref[0], cache[0], ahead[0], kx, sx)
    dkx[...] = jnp.zeros_like(dkx)
    dsx[...] = jnp.zeros_like(dsx)
    for number, block in enumerate((0, blocks - 1)):
        rows = block_rows(block)
        back_block(
            block, lambda pair: p_ref[number, pair], q_ref[0, rows], dmix_ref[rows], kx, sx, dq_ref, dkx, dsx
        )
    dq_ref[BLOCK : length - BLOCK] = jnp.zeros((length - 2 * BLOCK, dq_ref.shape[1]), F32)
    back_ref[:CACHE] = dkx[:CACHE]
    back_ref[CACHE:] = dsx[:SUMS]
    fore_ref[...] = dkx[CACHE + length :]


def back_inner_kernel(
    dmid, dmix, mix, q_ref, kv_ref, p_ref, dq_in, dkx_in, dsx_in,
    dq_ref, dkv_ref, dsum_ref, dwo_own, dwo_pair,
    kx, sx, dkx, dsx, dwo,
):
    length = dmid.shape[0]
    width = dwo_own.shape[1]
    blocks = length // BLOCK
    dwo[...] = mm(dmid[...], mix[...], 0, 0)
    dwo_own[...] = dwo[:, lanes_of(0, width)]
    dwo_pair[...] = dwo[:, lanes_of(1, width)]
    fill_keys(kv_ref[0], None, None, kx, sx)
    dq_ref[...] = dq_in[...]
    dkx[...] = dkx_in[...]
    dsx[...] = dsx_in[...]
    for number, block in enumerate(range(1, blocks - 1)):
        rows = block_rows(block)
        back_block(
            block, lambda pair: p_ref[0, number, pair], q_ref[0, rows], dmix[rows], kx, sx, dq_ref, dkx, dsx
        )
    dkv_ref[...] = dkx[CACHE : CACHE + length]
    dsum_ref[...] = dsx[SUMS : SUMS + length // SEG]


def feed_kernel(
    mix_own, mix_far, wo_own, wo_pair, wo_far, wo_far_pair, x_ref, g_ref, params,
    wi_own, wi_pair, bi_pair, wu_own, wu_pair,
    n2_ref, h_ref, dpre_ref, mid_ref, part_ref,
    mix, wo,
):
    width = wo_own.shape[0]
    hidden = wi_own.shape[1]
    far = far_bit()
    here = pl.multiple_of(far * 2 * width, 2 * width)
    there = pl.multiple_of((1 - far) * 2 * width, 2 * width)
    mix[:, pl.ds(here, 2 * width)] = mix_own[...]
    mix[:, pl.ds(there, 2 * width)] = mix_far[...]
    wo[lanes_of(0, width, here)] = wo_own[...]
    wo[lanes_of(1, width, here)] = wo_pair[...]
    wo[lanes_of(0, width, there)] = wo_far[...]
    wo[lanes_of(1, width, there)] = wo_far_pair[...]
    middle = x_ref[0] + mm(mix[...], wo[...]) + params[OUT_BIAS]
    mid_ref[...] = middle
    xhat, _ = normalise(middle)
    normed = xhat * params[SECOND_GAIN] + params[SECOND_SHIFT]
    n2_ref[...] = normed
    part = None
    for place, (wi, wu, bias) in enumerate(((wi_own, wu_own, params[INNER_BIAS]), (wi_pair, wu_pair, bi_pair[...]))):
        at = slice(place * hidden, (place + 1) * hidden)
        pre = mm(normed, wi[...]) + bias
        phi = 0.5 + 0.5 * lax.erf(pre * (0.5**0.5))
        h_ref[:, at] = pre * phi
        slope = phi + pre * (jnp.exp(-0.5 * pre * pre) * 0.3989422804014327)
        dpre = mm(g_ref[0], wu[...], 1, 1) * slope
        dpre_ref[:, at] = dpre
        step = mm(dpre, wi[...], 1, 1)
        part = step if part is None else part + step
    part_ref[...] = part


def put_rows(value, outs):
    at = 0
    for out in outs:
        count = out.shape[0]
        out[...] = value[at : at + count]
        at += count


def inner_weights_kernel(n2_0, n2_1, d_0, d_1, own_ref, *rest):
    *pair, vec_ref = rest
    hidden = own_ref.shape[1]
    for place, outs in enumerate(((own_ref,), pair)):
        at = slice(place * hidden, (place + 1) * hidden)
        put_rows(mm(n2_0[...], d_0[:, at], 0, 0) + mm(n2_1[...], d_1[:, at], 0, 0), outs)
        vec_ref[place : place + 1] = column_sums(d_0[:, at]) + column_sums(d_1[:, at])


def outer_weights_kernel(h_0, h_1, g_ref, own_ref, *rest):
    *pair, vec_ref = rest
    hidden = own_ref.shape[0]
    for place, outs in enumerate(((own_ref,), pair)):
        at = slice(place * hidden, (place + 1) * hidden)
        put_rows(mm(h_0[:, at], g_ref[0], 0, 0) + mm(h_1[:, at], g_ref[1], 0, 0), outs)
    vec_ref[...] = column_sums(g_ref[0]) + column_sums(g_ref[1])


def out_half_kernel(mid_ref, part, far, params, *outs):
    put_rows(mid_ref[...] + (part[...] + far[...]) + params[OUTER_BIAS], outs)


def feed_out_kernel(h_ref, wu_own, wu_pair, out_ref):
    hidden = wu_own.shape[0]
    out_ref[...] = mm(h_ref[:, :hidden], wu_own[...]) + mm(h_ref[:, hidden:], wu_pair[...])


def project_back_kernel(
    dq, dkv, dsum, cache_back, ahead_back, xhat, w_ref,
    dqkv_ref, part_ref, vec_ref, dsx,
):
    length, wide = dq.shape
    segs = length // SEG
    dsx[...] = dsum[...]
    dsx[segs - SUMS :] += cache_back[0, CACHE:]
    spread = jnp.broadcast_to((dsx[...] * (1.0 / SEG))[:, None, :], (segs, SEG, 2 * wide))
    dqkv_ref[:, :wide] = dq[...]
    dqkv_ref[:, wide:] = dkv[...] + spread.reshape(length, 2 * wide)
    dqkv_ref[length - CACHE :, wide:] += cache_back[0, :CACHE]
    dqkv_ref[:AHEAD, wide:] += ahead_back[0]
    part = mm(dqkv_ref[...], w_ref[...], 1, 1)
    part_ref[...] = part
    vec_ref[0:1] = column_sums(part * xhat[0])
    vec_ref[1:2] = column_sums(part)


def project_weights_kernel(
    normed, d_0, d_1, wo_own_0, wo_own_1, wo_pair_0, wo_pair_1, mid_0, mid_1, first_0, first_1, vec_outer, vec_inner,
    own_0, own_1, rows_ref, pair_rows, *rest,
):
    *pair, message, sums, row = rest
    features = normed.shape[2]
    width = wo_own_0.shape[1]
    hidden = vec_inner.shape[1]
    total = None
    for micro, grads in enumerate((d_0, d_1)):
        step = mm(normed[micro], grads[...], 0, 0)
        total = step if total is None else total + step
    sums[...] = total
    row[...] = column_sums(d_0[...]) + column_sums(d_1[...])
    rows_ref[0:3] = (mid_0[...] + mid_1[...]) * 0.5
    rows_ref[3:5] = first_0[...] + first_1[...]
    rows_ref[5:6] = vec_outer[...] * 0.5
    rows_ref[6:] = jnp.zeros((2, features), F32)
    pair_rows[0:6] = rows_ref[0:6]
    pair_rows[6:] = jnp.zeros((2, features), F32)
    for place, out_ref in enumerate((rows_ref, pair_rows)):
        for number in range(3):
            lanes = slice(number * width, (number + 1) * width)
            out_ref[6:7, lanes] = row[:, lanes_of(place, width, 2 * number * width)]
        out_ref[7:8, :hidden] = vec_inner[place : place + 1]
    for place, (outs, wo_0, wo_1) in enumerate((((own_0, own_1), wo_own_0, wo_own_1), (pair, wo_pair_0, wo_pair_1))):
        for number in range(3):
            lanes = slice(number * width, (number + 1) * width)
            message[:, lanes] = sums[:, lanes_of(place, width, 2 * number * width)]
        message[:, 3 * width :] = wo_0[...] + wo_1[...]
        put_rows(message, outs)


def frames_back_kernel(a_ref, b_ref, xhat, rate, dmid_ref, params, *outs):
    grad = norm_back(a_ref[...] + b_ref[...], params[FIRST_GAIN], xhat[0], rate[0, :, :1])
    put_rows(dmid_ref[...] + grad, outs)


def place_kernel(*refs):
    *pieces, out, sems = refs
    half = out.shape[1] // 2
    near = near_bit()
    pairs = []
    at = 0
    for piece in pieces:
        count = piece.shape[0]
        micro, at_half = at // (2 * half), at // half % 2
        start = (near + at_half * (1 - 2 * near)) * half + at % half
        pairs.append((piece, out.at[micro, pl.ds(pl.multiple_of(start, count), count)]))
        at += count
    for copy in copy_all(pairs, sems):
        copy.wait()


def place_of(bit):
    return lax.axis_index("tm") // bit % 2


def add_pieces(work, a_ref, pieces):
    at = 0
    for piece in pieces:
        count = piece.shape[0]
        work[at : at + count] = a_ref[at : at + count] + piece[...]
        at += count


def add_split_kernel(bit, rows, a_ref, *refs):
    if rows:
        rows_ref, *pieces, got_rows, mine_ref, theirs_ref, new_rows, work = refs
        new_rows[...] = rows_ref[...] + got_rows[...]
    else:
        *pieces, mine_ref, theirs_ref, work = refs
    half = mine_ref.shape[0]
    add_pieces(work, a_ref, pieces)
    place = place_of(bit)
    mine_ref[...] = work[pl.ds(pl.multiple_of(place * half, half), half)]
    theirs_ref[...] = work[pl.ds(pl.multiple_of((1 - place) * half, half), half)]


def add_kernel(rows, a_ref, *refs):
    if rows:
        rows_ref, *pieces, got_rows, out_ref, new_rows = refs
        new_rows[...] = rows_ref[...] + got_rows[...]
    else:
        *pieces, out_ref = refs
    add_pieces(out_ref, a_ref, pieces)


def join_kernel(bit, a_ref, b_ref, out_ref):
    half = a_ref.shape[0]
    place = place_of(bit)
    out_ref[pl.ds(pl.multiple_of(place * half, half), half)] = a_ref[...]
    out_ref[pl.ds(pl.multiple_of((1 - place) * half, half), half)] = b_ref[...]


def join_out_kernel(bit, a_ref, b_ref, out, sems):
    half = a_ref.shape[0]
    place = place_of(bit)
    pairs = [
        (a_ref, out.at[pl.ds(pl.multiple_of(place * half, half), half)]),
        (b_ref, out.at[pl.ds(pl.multiple_of((1 - place) * half, half), half)]),
    ]
    for copy in copy_all(pairs, sems):
        copy.wait()


def join_heads_kernel(bits, *refs):
    *parts, wq, wk, wv, wo = refs
    width = wq.shape[1]
    at = 0
    for number, bit in enumerate(bits):
        mine, theirs = parts[2 * number : 2 * number + 2]
        half = mine.shape[0]
        place = place_of(bit)
        for where, part in ((place, mine), (1 - place, theirs)):
            rows = pl.ds(pl.multiple_of(at + where * half, half), half)
            for heads, out in enumerate((wq, wk, wv)):
                out[rows, :] = part[:, heads * width : (heads + 1) * width]
            wo[:, rows] = part[:, 3 * width :].T
        at += 2 * half


def small_kernel(rows, far, *outs):
    width = outs[-3].shape[1]
    for number, out in enumerate(outs[:6]):
        out[...] = rows[number : number + 1] + far[number : number + 1]
    outs[6][...] = rows[6:7, :width]
    outs[7][...] = rows[6:7, 2 * width : 3 * width]
    outs[8][...] = rows[7:8, : outs[8].shape[1]]


def swap(value, axis, bit):
    size = lax.axis_size(axis)
    return lax.ppermute(value, axis, [(i, i ^ bit) for i in range(size)])


def swap_near(parts):
    return [swap(part, "head", 1) for part in parts]


def shift_halves(value, by):
    group = lax.axis_size("head")
    halves = 2 * lax.axis_size("tm")
    pairs = []
    for source in range(halves):
        target = source + by
        if 0 <= target < halves:
            for far in range(group // 2):
                place = lambda at: at // 2 * group + far * 2 + at % 2
                pairs.append((place(source), place(target)))
    return lax.ppermute(value, ("tm", "head"), pairs)


class SumOverTm:
    def __init__(self, run, a, b, first, rows=None):
        bits = [1 << i for i in range(lax.axis_size("tm").bit_length() - 1)]
        if first in bits:
            bits.remove(first)
            bits.insert(0, first)
        self.run, self.value, self.got = run, a, list(b)
        self.rows = [] if rows is None else [rows]
        self.down, self.last, self.up, self.place = bits[:-1], bits[-1:], bits[-2::-1], None
        self.step()

    def step(self):
        run, value = self.run, self.value
        count, features = value.shape
        has_rows = bool(self.rows)
        extra = [v.shape for v in self.rows]
        if self.down:
            bit = self.down.pop(0)
            half = (count // 2, features)
            self.value, message, *self.rows = run.call(
                functools.partial(add_split_kernel, bit, has_rows), "add_split", 0.1, [half, half] + extra,
                (value, *self.rows, *self.got), scratch=[value.shape],
            )
            self.got = [swap(v, "tm", bit) for v in (message, *self.rows)]
            return
        if self.place is None:
            self.value, *self.rows = run.call(
                functools.partial(add_kernel, has_rows), "add", 0.05, [value.shape] + extra,
                (value, *self.rows, *self.got),
            )
            if self.last:
                bit = self.last.pop()
                self.got = [swap(v, "tm", bit) for v in (self.value, *self.rows)]
                return
        else:
            (self.value,) = run.call(
                functools.partial(join_kernel, self.place), "join", 0.05, [(2 * count, features)], (value, *self.got)
            )
        self.place = self.up.pop(0)
        self.got = [swap(self.value, "tm", self.place)]

    @property
    def joined(self):
        return not self.up

    def halves(self):
        return (self.value, *self.got)


def per_device(
    frames, cotangent, seg_counts, query_weight, query_bias, key_weight, value_weight, value_bias,
    out_weight, out_bias, first_gain, first_shift, second_gain, second_shift,
    inner_weight, inner_bias, outer_weight, outer_bias,
):
    micro_count, shard, features = frames.shape
    width = query_weight.shape[1]
    hidden = inner_weight.shape[1]
    length = shard // 2
    segs = length // SEG
    blocks = length // BLOCK
    pairs = 2 * width // PAIR
    row = lambda v: v.reshape(1, v.shape[0])
    bq, bv, bo, bi, bu = map(row, (query_bias, value_bias, out_bias, inner_bias, outer_bias))
    g1, s1, g2, s2 = map(row, (first_gain, first_shift, second_gain, second_shift))
    big = (length, features)
    quarter = (length // 2, features)
    each = (micro_count, length)
    run = Steps()
    smem = pl.BlockSpec(memory_space=pltpu.SMEM)

    wq_pair, wk_pair, wv_pair, bq_pair, bv_pair = (
        swap(v, "head", 1) for v in (query_weight, key_weight, value_weight, bq, bv)
    )
    wo_far = swap(out_weight, "head", 2)

    x, xhat, rate, normed, w_own, b_own = run.call(
        norm_kernel, "norm", 0.8,
        [each + (features,)] * 2 + [each + (128,), each + (features,), (features, 3 * width), (1, 2 * width)],
        (frames, g1, s1, query_weight, key_weight, value_weight, bq, bv),
        scratch=[(16, features)], copies=micro_count + 7, far=range(8),
    )
    q, kv, tail, ahead, w_all, wi, wu, wo, g, params = run.call(
        project_kernel, "project", 2.2,
        [each + (2 * width,), each + (4 * width,),
         (micro_count, CACHE + SUMS, 4 * width), (micro_count, AHEAD, 4 * width), (features, 6 * width),
         inner_weight.shape, outer_weight.shape, out_weight.shape, each + (features,), (6, 1, features)],
        (normed, w_own, b_own, wq_pair, wk_pair, wv_pair, bq_pair, bv_pair,
         inner_weight, outer_weight, out_weight, cotangent, g1, g2, s2, bo, bi, bu),
        scratch=[(1, 6 * width)], copies=micro_count + 9, far=range(8, 18),
    )
    cache = shift_halves(tail, 1)
    ahead = shift_halves(ahead, -1)
    wo_pair, wi_pair, wu_pair, bi_pair = (swap(v, "head", 1) for v in (wo, wi, wu, params[INNER_BIAS]))

    key_scratch = [(CACHE + length + AHEAD, 4 * width), (SUMS + segs + SUMS, 4 * width)]
    q_spec = lambda m: micro_block((length, 2 * width), m)
    kv_spec = lambda m: micro_block((length, 4 * width), m)
    cache_spec = lambda m: micro_block((CACHE + SUMS, 4 * width), m)
    ahead_spec = lambda m: micro_block((AHEAD, 4 * width), m)
    square = (2 * BLOCK, KEYS)
    mix_inner, p_inner = run.call(
        attend_inner_kernel, "attend_inner", 3.7,
        [(micro_count, length - 2 * BLOCK, 2 * width), (micro_count, blocks - 2, pairs) + square],
        (seg_counts, q, kv), {0: smem}, key_scratch,
    )
    mix, mix_far, p_outer = [], [], []
    for m in range(micro_count):
        passed = [] if m else [wo_far]
        mix_m, p_m, *passed = run.call(
            functools.partial(attend_outer_kernel, m), "attend_outer", 2.05,
            [(length, 2 * width), (2, pairs) + square] + [v.shape for v in passed],
            (seg_counts, q, kv, cache, ahead, mix_inner, *passed),
            {0: smem, 1: q_spec(m), 2: kv_spec(m), 3: cache_spec(m), 4: ahead_spec(m),
             5: micro_block((length - 2 * BLOCK, 2 * width), m)},
            key_scratch,
        )
        mix.append(mix_m)
        mix_far.append(swap(mix_m, "head", 2))
        p_outer.append(p_m)
        if passed:
            wo_far_pair = swap(passed[0], "head", 1)
    feed, dn2 = [], []
    for m in range(micro_count):
        feed.append(run.call(
            feed_kernel, "feed", 3.9,
            [big, (length, 2 * hidden), (length, 2 * hidden), big, big],
            (mix[m], mix_far[m], wo, wo_pair, wo_far, wo_far_pair, x, g, params, wi, wi_pair, bi_pair, wu, wu_pair),
            {6: micro_block(big, m), 7: micro_block(big, m)},
            [(length, features), (features, features)],
        ))
        dn2.append((feed[m][4], swap(feed[m][4], "head", 2)))

    def feed_out(m):
        (part,) = run.call(feed_out_kernel, "feed_out", 1.1, [big], (feed[m][1], wu, wu_pair))
        return part, swap(part, "head", 2)

    def out_half(m):
        half = run.call(out_half_kernel, "out_half", 0.1, [quarter] * 2, (feed[m][3], *parts[m], params))
        return [*half, *swap_near(half)]

    def back_outer(m):
        return run.call(
            back_outer_kernel, "back_outer", 2.7,
            [big, (length, 2 * width), (length, 2 * width), (CACHE + SUMS, 4 * width), (AHEAD, 4 * width), (3, features)]
            + key_scratch,
            (*dn2[m], feed[m][3], g, params, wo, wo_pair, q, kv, cache, ahead, p_outer[m]),
            {3: micro_block(big, m), 7: q_spec(m), 8: kv_spec(m), 9: cache_spec(m), 10: ahead_spec(m)},
            key_scratch,
        )

    def back_inner(m):
        dmid, dmix, dq, _, _, _, dkx, dsx = outers[m]
        return run.call(
            back_inner_kernel, "back_inner", 1.9,
            [(length, 2 * width), (length, 4 * width), (segs, 4 * width), (features, width), (features, width)],
            (dmid, dmix, mix[m], q, kv, p_inner, dq, dkx, dsx),
            {3: q_spec(m), 4: kv_spec(m), 5: micro_block((blocks - 2, pairs) + square, m)},
            key_scratch * 2 + [(features, 2 * width)],
        )

    def project_back(m):
        dq, dkv, dsum, _, _ = inners[m]
        return run.call(
            project_back_kernel, "project_back", 0.9,
            [(length, 6 * width), big, (2, features)],
            (dq, dkv, dsum, cache_back, ahead_back, xhat, w_all),
            {3: cache_spec(m), 4: ahead_spec(m), 5: micro_block(big, m)},
            [(segs, 4 * width)],
        )

    def frames_back(m):
        half = run.call(
            frames_back_kernel, "frames_back", 0.3, [quarter] * 2,
            (*dn1[m], xhat, rate, outers[m][0], params),
            {2: micro_block(big, m), 3: micro_block((length, 128), m)},
        )
        return [*half, *swap_near(half)]

    def place(halves):
        args = [half for both in halves for half in both]
        (out,) = run.call(
            place_kernel, "place", 1.3, [(micro_count, 2 * length, features)], args, copies=len(args), far_outs=[0],
        )
        return out

    inner_own, *inner_pair, vec_inner = run.call(
        inner_weights_kernel, "inner_weights", 2.0,
        [(features, hidden)] + [(features // 4, hidden)] * 4 + [(2, hidden)],
        (feed[0][0], feed[1][0], feed[0][2], feed[1][2]),
    )
    inner_pair = swap_near(inner_pair)
    outer_own, *outer_pair, vec_outer = run.call(
        outer_weights_kernel, "outer_weights", 1.95,
        [(hidden, features)] + [(hidden // 4, features)] * 4 + [(1, features)],
        (feed[0][1], feed[1][1], g),
    )
    outer_pair = swap_near(outer_pair)
    parts, outers, inners, fronts, dn1, outs, halves = [], [], [], [], [], [], []
    parts.append(feed_out(0))
    inner = SumOverTm(run, inner_own, inner_pair, 2)
    outer = SumOverTm(run, outer_own, outer_pair, 1)
    outers.append(back_outer(0))
    inners.append(back_inner(0))
    outers.append(back_outer(1))
    cache_back = shift_halves(jnp.stack([outers[0][3], outers[1][3]]), -1)
    ahead_back = shift_halves(jnp.stack([outers[0][4], outers[1][4]]), 1)
    inners.append(back_inner(1))
    parts.append(feed_out(1))
    inner.step()
    outer.step()
    outs.append(out_half(0))
    for m in range(micro_count):
        fronts.append(project_back(m))
        dn1.append((fronts[m][1], swap(fronts[m][1], "head", 2)))
    attn_0, attn_1, rows, pair_rows, *attn_pair = run.call(
        project_weights_kernel, "project_weights", 1.8,
        [(features // 2, 4 * width)] * 2 + [(8, features)] * 2 + [(features // 4, 4 * width)] * 4,
        (normed, fronts[0][0], fronts[1][0], inners[0][3], inners[1][3], inners[0][4], inners[1][4],
         outers[0][5], outers[1][5], fronts[0][2], fronts[1][2], vec_outer, vec_inner),
        scratch=[(features, 4 * width), (features, 6 * width), (1, 6 * width)],
    )
    *attn_pair, pair_rows = swap_near([*attn_pair, pair_rows])
    inner.step()
    outer.step()
    attn_0 = SumOverTm(run, attn_0, [*attn_pair[:2], pair_rows], 1, rows)
    attn_1 = SumOverTm(run, attn_1, attn_pair[2:], 2)
    outs.append(out_half(1))
    attn_0.step()
    attn_1.step()
    layer_output = place(outs)
    halves.append(frames_back(0))
    inner.step()
    outer.step()
    attn_0.step()
    attn_1.step()
    halves.append(frames_back(1))
    inner.step()
    outer.step()
    frames_grad = place(halves)
    chains = (attn_0, attn_1, inner, outer)
    while not all(chain.joined for chain in chains):
        for chain in chains:
            if not chain.joined:
                chain.step()
    square_out = dict(copies=2, far_outs=[0])
    (inner_grad,) = run.call(
        functools.partial(join_out_kernel, inner.place), "join_out", 1.0, [inner_weight.shape], inner.halves(), **square_out
    )
    (outer_grad,) = run.call(
        functools.partial(join_out_kernel, outer.place), "join_out", 1.0, [outer_weight.shape], outer.halves(), **square_out
    )
    small = run.call(
        small_kernel, "small", 0.6, [(1, features)] * 6 + [(1, width)] * 2 + [(1, hidden)],
        (attn_0.rows[0], swap(attn_0.rows[0], "head", 2)),
    )
    weights = run.call(
        functools.partial(join_heads_kernel, (attn_0.place, attn_1.place)), "join_heads", 1.0,
        [(features, width)] * 3 + [(width, features)], (*attn_0.halves(), *attn_1.halves()),
    )
    bo, g2, s2, g1, s1, bu, bq, bv, bi = (v.reshape(v.shape[1]) for v in small)
    return (
        layer_output, frames_grad, weights[0], bq, weights[1], weights[2], bv, weights[3], bo,
        g1, s1, g2, s2, inner_grad, bi, outer_grad, bu,
    )


def solution(mesh):
    in_specs = (
        P(None, "tm", None),
        P(None, "tm", None),
        P(),
        P(None, "head"),
        P("head"),
        P(None, "head"),
        P(None, "head"),
        P("head"),
        P("head", None),
        P(),
        P(),
        P(),
        P(),
        P(),
        P(None, "head"),
        P("head"),
        P("head", None),
        P(),
    )
    out_specs = (
        P(None, "tm", None),
        P(None, "tm", None),
        P(None, "head"),
        P("head"),
        P(None, "head"),
        P(None, "head"),
        P("head"),
        P("head", None),
        P(),
        P(),
        P(),
        P(),
        P(),
        P(None, "head"),
        P("head"),
        P("head", None),
        P(),
    )
    return jax.shard_map(
        per_device, mesh=mesh, in_specs=in_specs, out_specs=out_specs, check_vma=False
    )
```

time: 691 us -> 181 us (0.26); the launches traced: 679 us -> 178 us
  waiting for transfers between devices: 240 us -> 65.7 us
  local copies, waits for them, and re-layouts: 150 us -> 0.7 us
  matrix products: 135 us -> 0 us
  other arithmetic: 71.9 us -> 0.02 us
  Pallas kernels: 0 us -> 48.4 us
  blocking collectives: 39.5 us -> 0 us
  starting transfers between devices: 26.8 us -> 61.1 us
  between operations: 16 us -> 1.7 us
    psum x4 -> x0, waiting for transfers between devices: 240 us -> none  [the longest x1 86.7 us: per_device(): lax.psum((steps_now[0], steps_now[1], steps_now[2], steps_now[3], steps_n...]
    dot_general x48 -> x0, matrix products: 135 us -> none  [the longest x36 86.3 us: product(): return jnp.dot(left, right, precision=HIGHEST)]
    ppermute x8 -> x68, waiting for transfers between devices: 0.02 us -> 65.7 us  [the longest x64 65.7 us: swap(): return lax.ppermute(value, axis, [(i, i ^ bit) for i in range(size)])]
    pallas_call x0 -> x48, Pallas kernels: none -> 48.4 us  [call(): pl.pallas_call(body, name=name, grid=(1,), in_specs=[in_hbm if i in far e...]
    reshape x16 -> x0, local copies, waits for them, and re-layouts: 42.2 us -> none  [the longest x4 13 us: attend(): keyset[:, :, feature_width:]]
    psum x1 -> x0, blocking collectives: 39.5 us -> none  [per_device(): lax.psum((steps_now[0], steps_now[1], steps_now[2], steps_now[3], steps_n...]
    slice x23 -> x0, local copies, waits for them, and re-layouts: 36.1 us -> none  [the longest x11 21.7 us: attend(): blocks[i:i + seg_count]]
    ppermute x8 -> x68, starting transfers between devices: 25.8 us -> 61.1 us  [the longest x64 52 us: swap(): return lax.ppermute(value, axis, [(i, i ^ bit) for i in range(size)])]
  transfers between devices with their start and end apart: 12 -> 68, of which waited for: 4 -> 19; matrix products, arithmetic and copies ran while one was open for 23% -> 0% of each run, Pallas kernels for 0% -> 21%
where the time goes in v1:
time: 181 us; the launch traced here: 178 us
  waiting for transfers between devices  65.7 us (36%)
  starting transfers between devices  61.1 us (34%)
  Pallas kernels  48.4 us (27%)
    ppermute x64, waiting for transfers between devices, swap(): return lax.ppermute(value, axis, [(i, i ^ bit) for i in range(size)])  65.7 us
    ppermute x64, starting transfers between devices, swap(): return lax.ppermute(value, axis, [(i, i ^ bit) for i in range(size)])  52 us
    pallas_call x48, Pallas kernels, call(): pl.pallas_call(body, name=name, grid=(1,), in_specs=[in_hbm if i in far e...  48.4 us
    ppermute x4, starting transfers between devices, shift_halves(): return lax.ppermute(value, ('tm', 'head'), pairs)  9.07 us
  transfers between devices with their start and end apart: 68, of which 19 were waited for; matrix products, arithmetic and copies ran while one was open for 0% of the time, Pallas kernels for 21%

profile of v1, /device:TPU:0, one launch (start us, length us, event | category | flops | bytes accessed | tf_op | source)
XLA Modules:
  0.0 177.7 jit_solution(951899686711009934)
XLA Ops:
  3.9 3.8 %project.1 = (f32[2,256,256]{2,1,0:T(8,128)S(1)}, f32[2,256,512]{2,1,0:T(8,128)S(1)}, f32[2,40,512]{2,1,0:T(8,128)S(1)}, f32[2,8,512]{2,1,0:T(8,128)S(1)}, f32[5...) custom-call(f32[2,256,512]{2,1,0:T(8,128)S(1)} %get-tuple-element.15, ...), custom_call_target="tpu_custom_call" | custom-call | flops 1139600000 | tf_op jit(solution)/shard_map/project/pallas_call | solution.py:119
  12.2 3.2 %collective-permute-start.5 = (f32[2,40,512]{2,1,0:T(8,128)S(1)}, f32[2,40,512]{2,1,0:T(8,128)S(1)}, u32[]{:S(2)}, u32[]{:S(2)}) collective-permute-start(f32[2,40,512]{2,1,0:T(8,128)S(1)} %get-tuple-element.158), channel_id=1, source_target_pairs={{0,1},{2,3},{1,4},{3,6},{4,5},{6,7},{5,8},{7,10},{8,9},{10,11},{9,... | collective-permute-start | bytes 491528 | tf_op jit(solution)/shard_map/ppermute | solution.py:636
  15.4 3.7 %attend_inner.1 = (f32[2,128,256]{2,1,0:T(8,128)S(1)}, f32[2,2,2,128,128]{4,3,2,1,0:T(8,128)S(1)}) custom-call(s32[2,4]{1,0:T(2,128)S(1)} %copy-done, f32[2,256,256]{2,1,0:T(8,128)S(1)} %get-tuple-element.156.refs_1_.refs_7_.refs_3_, f32[2,256,512]{2,1,0:T(8,128)S(1)} %get-tuple-element.157.refs_2_.refs_8_.refs_4_, ...), custom_call_target="tpu_custom_call" | custom-call | flops 1916600064 | tf_op jit(solution)/shard_map/attend_inner/pallas_call | solution.py:119
  27.4 5.0 %collective-permute-done.8.refs_1_ = f32[256,256]{1,0:T(8,128)S(1)} collective-permute-done((f32[256,256]{1,0:T(8,128)S(1)}, f32[256,256]{1,0:T(8,128)S(1)}, u32[]{:S(2)}, u32[]{:S(2)}) %collective-permute-start.8) | collective-permute-done | bytes 262176 | tf_op jit(solution)/shard_map/ppermute | solution.py:619
  32.4 3.9 %feed.2 = (f32[256,512]{1,0:T(8,128)S(1)}, f32[256,1024]{1,0:T(8,128)S(1)}, f32[256,1024]{1,0:T(8,128)S(1)}, f32[256,512]{1,0:T(8,128)S(1)}, f32[256,512]{1,0:T(8,128)S(1)}) custom-call(f32[256,256]{1,0:T(8,128)S(1)} %get-tuple-element.163.refs_0_.refs_2_, f32[256,256]{1,0:T(8,128)S(1)} %collective-permute-done.8.refs_1_, ...), custom_call_target="tpu_custom_call" | custom-call | flops 2020199936 | tf_op jit(solution)/shard_map/feed/pallas_call | solution.py:119
  37.2 3.9 %feed.3 = (f32[256,512]{1,0:T(8,128)S(1)}, f32[256,1024]{1,0:T(8,128)S(1)}, f32[256,1024]{1,0:T(8,128)S(1)}, f32[256,512]{1,0:T(8,128)S(1)}, f32[256,512]{1,0:T(8,128)S(1)}) custom-call(f32[256,256]{1,0:T(8,128)S(1)} %get-tuple-element.173.refs_0_.refs_2_, f32[256,256]{1,0:T(8,128)S(1)} %collective-permute-done.14.refs_1_, ...), custom_call_target="tpu_custom_call" | custom-call | flops 2020199936 | tf_op jit(solution)/shard_map/feed/pallas_call | solution.py:119
  50.7 2.6 %collective-permute-start.25 = (f32[256,512]{1,0:T(8,128)S(1)}, f32[256,512]{1,0:T(8,128)S(1)}, u32[]{:S(2)}, u32[]{:S(2)}) collective-permute-start(f32[256,512]{1,0:T(8,128)S(1)} %get-tuple-element.193.refs_5_), channel_id=1, source_target_pairs={{0,8},{4,12},{8,0},{12,4},{16,24},{20,28},{24,16},{28,20},{1,9},{5... | collective-permute-start | bytes 1572872 | tf_op jit(solution)/shard_map/ppermute | solution.py:619
  55.1 6.0 %collective-permute-done.27.refs_1_ = f32[256,512]{1,0:T(8,128)S(1)} collective-permute-done((f32[256,512]{1,0:T(8,128)S(1)}, f32[256,512]{1,0:T(8,128)S(1)}, u32[]{:S(2)}, u32[]{:S(2)}) %collective-permute-start.27) | collective-permute-done | bytes 524320 | tf_op jit(solution)/shard_map/ppermute | solution.py:619
  61.1 2.7 %back_outer.2 = (f32[256,512]{1,0:T(8,128)S(1)}, f32[256,256]{1,0:T(8,128)S(1)}, f32[256,256]{1,0:T(8,128)S(1)}, f32[40,512]{1,0:T(8,128)S(1)}, f32[8,512]{1,0:T...) custom-call(f32[256,512]{1,0:T(8,128)S(1)} %get-tuple-element.174.refs_14_.refs_0_, ...), custom_call_target="tpu_custom_call" | custom-call | flops 1398599936 | tf_op jit(solution)/shard_map/back_outer/pallas_call | solution.py:119
  65.8 6.6 %collective-permute-done.26.refs_1_ = f32[256,512]{1,0:T(8,128)S(1)} collective-permute-done((f32[256,512]{1,0:T(8,128)S(1)}, f32[256,512]{1,0:T(8,128)S(1)}, u32[]{:S(2)}, u32[]{:S(2)}) %collective-permute-start.26) | collective-permute-done | bytes 524320 | tf_op jit(solution)/shard_map/ppermute | solution.py:619
  72.4 2.7 %back_outer.3 = (f32[256,512]{1,0:T(8,128)S(1)}, f32[256,256]{1,0:T(8,128)S(1)}, f32[256,256]{1,0:T(8,128)S(1)}, f32[40,512]{1,0:T(8,128)S(1)}, f32[8,512]{1,0:T...) custom-call(f32[256,512]{1,0:T(8,128)S(1)} %get-tuple-element.180.refs_4_.refs_0_, ...), custom_call_target="tpu_custom_call" | custom-call | flops 1398599936 | tf_op jit(solution)/shard_map/back_outer/pallas_call | solution.py:119
  76.4 3.3 %collective-permute-start.32 = (f32[2,8,512]{2,1,0:T(8,128)S(1)}, f32[2,8,512]{2,1,0:T(8,128)S(1)}, u32[]{:S(2)}, u32[]{:S(2)}) collective-permute-start(f32[2,8,512]{2,1,0:T(8,128)S(1)} %pad_maximum_fusion.1), channel_id=1, source_target_pairs={{0,1},{2,3},{1,4},{3,6},{4,5},{6,7},{5,8},{7,10},{8,9},{10,11},{9,... | collective-permute-start | bytes 98312 | tf_op jit(solution)/shard_map/ppermute | solution.py:636
  83.2 2.7 %collective-permute-start.39 = (f32[128,512]{1,0:T(8,128)S(1)}, f32[128,512]{1,0:T(8,128)S(1)}, u32[]{:S(2)}, u32[]{:S(2)}) collective-permute-start(f32[128,512]{1,0:T(8,128)S(1)} %get-tuple-element.211.refs_2_), channel_id=1, source_target_pairs={{0,4},{4,0},{8,12},{12,8},{16,20},{20,16},{24,28},{28,24},{1,5},{5... | collective-permute-start | bytes 786440 | tf_op jit(solution)/shard_map/ppermute | solution.py:619
  102.1 3.1 %collective-permute-done.44.refs_3_ = f32[8,512]{1,0:T(8,128)S(1)} collective-permute-done((f32[8,512]{1,0:T(8,128)S(1)}, f32[8,512]{1,0:T(8,128)S(1)}, u32[]{:S(2)}, u32[]{:S(2)}) %collective-permute-start.44) | collective-permute-done | bytes 16416 | tf_op jit(solution)/shard_map/ppermute | solution.py:619
  106.8 2.6 %collective-permute-start.53 = (f32[128,512]{1,0:T(8,128)S(1)}, f32[128,512]{1,0:T(8,128)S(1)}, u32[]{:S(2)}, u32[]{:S(2)}) collective-permute-start(f32[128,512]{1,0:T(8,128)S(1)} %add.8.refs_2_.refs_0_), channel_id=1, source_target_pairs={{0,16},{4,20},{8,24},{12,28},{16,0},{20,4},{24,8},{28,12},{1,17},{... | collective-permute-start | bytes 786440 | tf_op jit(solution)/shard_map/ppermute | solution.py:619
  113.2 14.9 %collective-permute-done.53.refs_1_ = f32[128,512]{1,0:T(8,128)S(1)} collective-permute-done((f32[128,512]{1,0:T(8,128)S(1)}, f32[128,512]{1,0:T(8,128)S(1)}, u32[]{:S(2)}, u32[]{:S(2)}) %collective-permute-start.53) | collective-permute-done | bytes 262176 | tf_op jit(solution)/shard_map/ppermute | solution.py:619
  130.2 2.8 %collective-permute-done.52.refs_1_ = f32[128,512]{1,0:T(8,128)S(1)} collective-permute-done((f32[128,512]{1,0:T(8,128)S(1)}, f32[128,512]{1,0:T(8,128)S(1)}, u32[]{:S(2)}, u32[]{:S(2)}) %collective-permute-start.52) | collective-permute-done | bytes 262176 | tf_op jit(solution)/shard_map/ppermute | solution.py:619
  133.0 3.7 %collective-permute-done.51.refs_3_ = f32[8,512]{1,0:T(8,128)S(1)} collective-permute-done((f32[8,512]{1,0:T(8,128)S(1)}, f32[8,512]{1,0:T(8,128)S(1)}, u32[]{:S(2)}, u32[]{:S(2)}) %collective-permute-start.51) | collective-permute-done | bytes 16416 | tf_op jit(solution)/shard_map/ppermute | solution.py:619
  138.9 4.6 %collective-permute-done.56.refs_1_ = f32[128,512]{1,0:T(8,128)S(1)} collective-permute-done((f32[128,512]{1,0:T(8,128)S(1)}, f32[128,512]{1,0:T(8,128)S(1)}, u32[]{:S(2)}, u32[]{:S(2)}) %collective-permute-start.56) | collective-permute-done | bytes 262176 | tf_op jit(solution)/shard_map/ppermute | solution.py:619
  144.0 3.3 %collective-permute-start.58 = (f32[64,512]{1,0:T(8,128)S(1)}, f32[64,512]{1,0:T(8,128)S(1)}, u32[]{:S(2)}, u32[]{:S(2)}) collective-permute-start(f32[64,512]{1,0:T(8,128)S(1)} %get-tuple-element.268.refs_0_), channel_id=1, source_target_pairs={{0,16},{4,20},{8,24},{12,28},{16,0},{20,4},{24,8},{28,12},{1,17},{... | collective-permute-start | bytes 393224 | tf_op jit(solution)/shard_map/ppermute | solution.py:619
  147.3 2.9 %collective-permute-start.59 = (f32[8,512]{1,0:T(8,128)S(1)}, f32[8,512]{1,0:T(8,128)S(1)}, u32[]{:S(2)}, u32[]{:S(2)}) collective-permute-start(f32[8,512]{1,0:T(8,128)S(1)} %get-tuple-element.264.refs_2_.refs_1_), channel_id=1, source_target_pairs={{0,16},{4,20},{8,24},{12,28},{16,0},{20,4},{24,8},{28,12},{1,17},{... | collective-permute-start | bytes 49160 | tf_op jit(solution)/shard_map/ppermute | solution.py:619
  151.6 7.9 %collective-permute-done.59.refs_3_ = f32[8,512]{1,0:T(8,128)S(1)} collective-permute-done((f32[8,512]{1,0:T(8,128)S(1)}, f32[8,512]{1,0:T(8,128)S(1)}, u32[]{:S(2)}, u32[]{:S(2)}) %collective-permute-start.59) | collective-permute-done | bytes 16416 | tf_op jit(solution)/shard_map/ppermute | solution.py:619
  161.9 2.7 %collective-permute-start.63 = (f32[64,512]{1,0:T(8,128)S(1)}, f32[64,512]{1,0:T(8,128)S(1)}, u32[]{:S(2)}, u32[]{:S(2)}) collective-permute-start(f32[64,512]{1,0:T(8,128)S(1)} %add.15.refs_2_.refs_0_), channel_id=1, source_target_pairs={{0,4},{4,0},{8,12},{12,8},{16,20},{20,16},{24,28},{28,24},{1,5},{5... | collective-permute-start | bytes 393224 | tf_op jit(solution)/shard_map/ppermute | solution.py:619
  165.8 3.1 %collective-permute-done.63.refs_1_ = f32[64,512]{1,0:T(8,128)S(1)} collective-permute-done((f32[64,512]{1,0:T(8,128)S(1)}, f32[64,512]{1,0:T(8,128)S(1)}, u32[]{:S(2)}, u32[]{:S(2)}) %collective-permute-start.63) | collective-permute-done | bytes 131104 | tf_op jit(solution)/shard_map/ppermute | solution.py:619
  (169 shorter events, 74.4 us)
Async XLA Ops:
  7.7 24.7 %collective-permute-start.11 = (f32[512,512]{1,0:T(8,128)S(1)}, f32[512,512]{1,0:T(8,128)S(1)}, u32[]{:S(2)}, u32[]{:S(2)}) collective-permute-start(f32[512,512]{1,0:T(8,128)S(1)} %get-tuple-element.168.refs_9_), channel_id=1, source_target_pairs={{0,1},{1,0},{2,3},{3,2},{4,5},{5,4},{6,7},{7,6},{8,9},{9,8},{10,11... | collective-permute-start | bytes 3145736 | tf_op jit(solution)/shard_map/ppermute | solution.py:619
  7.9 24.6 %collective-permute-start.13 = (f32[512,512]{1,0:T(8,128)S(1)}, f32[512,512]{1,0:T(8,128)S(1)}, u32[]{:S(2)}, u32[]{:S(2)}) collective-permute-start(f32[512,512]{1,0:T(8,128)S(1)} %get-tuple-element.169.refs_12_.refs_1_), channel_id=1, source_target_pairs={{0,1},{1,0},{2,3},{3,2},{4,5},{5,4},{6,7},{7,6},{8,9},{9,8},{10,11... | collective-permute-start | bytes 3145736 | tf_op jit(solution)/shard_map/ppermute | solution.py:619
  8.3 10.8 %collective-permute-start.7 = (f32[128,512]{1,0:T(8,128)S(1)}, f32[128,512]{1,0:T(8,128)S(1)}, u32[]{:S(2)}, u32[]{:S(2)}) collective-permute-start(f32[128,512]{1,0:T(8,128)S(1)} %copy-done.2), channel_id=1, source_target_pairs={{0,2},{1,3},{2,0},{3,1},{4,6},{5,7},{6,4},{7,5},{8,10},{9,11},{10,... | collective-permute-start | bytes 786440 | tf_op jit(solution)/shard_map/ppermute | solution.py:619
  25.6 11.6 %collective-permute-start.14 = (f32[256,256]{1,0:T(8,128)S(1)}, f32[256,256]{1,0:T(8,128)S(1)}, u32[]{:S(2)}, u32[]{:S(2)}) collective-permute-start(f32[256,256]{1,0:T(8,128)S(1)} %get-tuple-element.173.refs_0_.refs_2_), channel_id=1, source_target_pairs={{0,2},{1,3},{2,0},{3,1},{4,6},{5,7},{6,4},{7,5},{8,10},{9,11},{10,... | collective-permute-start | bytes 786440 | tf_op jit(solution)/shard_map/ppermute | solution.py:619
  46.4 14.7 %collective-permute-start.27 = (f32[256,512]{1,0:T(8,128)S(1)}, f32[256,512]{1,0:T(8,128)S(1)}, u32[]{:S(2)}, u32[]{:S(2)}) collective-permute-start(f32[256,512]{1,0:T(8,128)S(1)} %get-tuple-element.174.refs_14_.refs_0_), channel_id=1, source_target_pairs={{0,2},{1,3},{2,0},{3,1},{4,6},{5,7},{6,4},{7,5},{8,10},{9,11},{10,... | collective-permute-start | bytes 1572872 | tf_op jit(solution)/shard_map/ppermute | solution.py:619
  46.7 25.7 %collective-permute-start.26 = (f32[256,512]{1,0:T(8,128)S(1)}, f32[256,512]{1,0:T(8,128)S(1)}, u32[]{:S(2)}, u32[]{:S(2)}) collective-permute-start(f32[256,512]{1,0:T(8,128)S(1)} %get-tuple-element.180.refs_4_.refs_0_), channel_id=1, source_target_pairs={{0,2},{1,3},{2,0},{3,1},{4,6},{5,7},{6,4},{7,5},{8,10},{9,11},{10,... | collective-permute-start | bytes 1572872 | tf_op jit(solution)/shard_map/ppermute | solution.py:619
  50.3 35.6 %collective-permute-start.15 = (f32[256,512]{1,0:T(8,128)S(1)}, f32[256,512]{1,0:T(8,128)S(1)}, u32[]{:S(2)}, u32[]{:S(2)}) collective-permute-start(f32[256,512]{1,0:T(8,128)S(1)} %feed_out.2.refs_5_.refs_1_), channel_id=1, source_target_pairs={{0,2},{1,3},{2,0},{3,1},{4,6},{5,7},{6,4},{7,5},{8,10},{9,11},{10,... | collective-permute-start | bytes 1572872 | tf_op jit(solution)/shard_map/ppermute | solution.py:619
  50.7 32.0 %collective-permute-start.25 = (f32[256,512]{1,0:T(8,128)S(1)}, f32[256,512]{1,0:T(8,128)S(1)}, u32[]{:S(2)}, u32[]{:S(2)}) collective-permute-start(f32[256,512]{1,0:T(8,128)S(1)} %get-tuple-element.193.refs_5_), channel_id=1, source_target_pairs={{0,8},{4,12},{8,0},{12,4},{16,24},{20,28},{24,16},{28,20},{1,9},{5... | collective-permute-start | bytes 1572872 | tf_op jit(solution)/shard_map/ppermute | solution.py:619
  53.5 29.7 %collective-permute-start.24 = (f32[256,512]{1,0:T(8,128)S(1)}, f32[256,512]{1,0:T(8,128)S(1)}, u32[]{:S(2)}, u32[]{:S(2)}) collective-permute-start(f32[256,512]{1,0:T(8,128)S(1)} %get-tuple-element.195.refs_12_), channel_id=1, source_target_pairs={{0,4},{4,0},{8,12},{12,8},{16,20},{20,16},{24,28},{28,24},{1,5},{5... | collective-permute-start | bytes 1572872 | tf_op jit(solution)/shard_map/ppermute | solution.py:619
  75.1 12.6 %collective-permute-start.31 = (f32[2,40,512]{2,1,0:T(8,128)S(1)}, f32[2,40,512]{2,1,0:T(8,128)S(1)}, u32[]{:S(2)}, u32[]{:S(2)}) collective-permute-start(f32[2,40,512]{2,1,0:T(8,128)S(1)} %pad_maximum_fusion), channel_id=1, source_target_pairs={{1,0},{3,2},{4,1},{6,3},{5,4},{7,6},{8,5},{10,7},{9,8},{11,10},{12... | collective-permute-start | bytes 491528 | tf_op jit(solution)/shard_map/ppermute | solution.py:636
  76.4 11.3 %collective-permute-start.32 = (f32[2,8,512]{2,1,0:T(8,128)S(1)}, f32[2,8,512]{2,1,0:T(8,128)S(1)}, u32[]{:S(2)}, u32[]{:S(2)}) collective-permute-start(f32[2,8,512]{2,1,0:T(8,128)S(1)} %pad_maximum_fusion.1), channel_id=1, source_target_pairs={{0,1},{2,3},{1,4},{3,6},{4,5},{6,7},{5,8},{7,10},{8,9},{10,11},{9,... | collective-permute-start | bytes 98312 | tf_op jit(solution)/shard_map/ppermute | solution.py:636
  82.7 15.8 %collective-permute-start.30 = (f32[256,512]{1,0:T(8,128)S(1)}, f32[256,512]{1,0:T(8,128)S(1)}, u32[]{:S(2)}, u32[]{:S(2)}) collective-permute-start(f32[256,512]{1,0:T(8,128)S(1)} %feed_out.3.refs_2_.refs_1_), channel_id=1, source_target_pairs={{0,2},{1,3},{2,0},{3,1},{4,6},{5,7},{6,4},{7,5},{8,10},{9,11},{10,... | collective-permute-start | bytes 1572872 | tf_op jit(solution)/shard_map/ppermute | solution.py:619
  83.2 11.8 %collective-permute-start.39 = (f32[128,512]{1,0:T(8,128)S(1)}, f32[128,512]{1,0:T(8,128)S(1)}, u32[]{:S(2)}, u32[]{:S(2)}) collective-permute-start(f32[128,512]{1,0:T(8,128)S(1)} %get-tuple-element.211.refs_2_), channel_id=1, source_target_pairs={{0,4},{4,0},{8,12},{12,8},{16,20},{20,16},{24,28},{28,24},{1,5},{5... | collective-permute-start | bytes 786440 | tf_op jit(solution)/shard_map/ppermute | solution.py:619
  96.9 15.9 %collective-permute-start.45 = (f32[256,512]{1,0:T(8,128)S(1)}, f32[256,512]{1,0:T(8,128)S(1)}, u32[]{:S(2)}, u32[]{:S(2)}) collective-permute-start(f32[256,512]{1,0:T(8,128)S(1)} %get-tuple-element.255.refs_0_), channel_id=1, source_target_pairs={{0,2},{1,3},{2,0},{3,1},{4,6},{5,7},{6,4},{7,5},{8,10},{9,11},{10,... | collective-permute-start | bytes 1572872 | tf_op jit(solution)/shard_map/ppermute | solution.py:619
  105.2 32.6 %collective-permute-start.48 = (f32[256,512]{1,0:T(8,128)S(1)}, f32[256,512]{1,0:T(8,128)S(1)}, u32[]{:S(2)}, u32[]{:S(2)}) collective-permute-start(f32[256,512]{1,0:T(8,128)S(1)} %get-tuple-element.260.refs_0_), channel_id=1, source_target_pairs={{0,2},{1,3},{2,0},{3,1},{4,6},{5,7},{6,4},{7,5},{8,10},{9,11},{10,... | collective-permute-start | bytes 1572872 | tf_op jit(solution)/shard_map/ppermute | solution.py:619
  106.8 21.3 %collective-permute-start.53 = (f32[128,512]{1,0:T(8,128)S(1)}, f32[128,512]{1,0:T(8,128)S(1)}, u32[]{:S(2)}, u32[]{:S(2)}) collective-permute-start(f32[128,512]{1,0:T(8,128)S(1)} %add.8.refs_2_.refs_0_), channel_id=1, source_target_pairs={{0,16},{4,20},{8,24},{12,28},{16,0},{20,4},{24,8},{28,12},{1,17},{... | collective-permute-start | bytes 786440 | tf_op jit(solution)/shard_map/ppermute | solution.py:619
  109.4 23.6 %collective-permute-start.52 = (f32[128,512]{1,0:T(8,128)S(1)}, f32[128,512]{1,0:T(8,128)S(1)}, u32[]{:S(2)}, u32[]{:S(2)}) collective-permute-start(f32[128,512]{1,0:T(8,128)S(1)} %add.9.refs_5_.refs_0_), channel_id=1, source_target_pairs={{0,16},{4,20},{8,24},{12,28},{16,0},{20,4},{24,8},{28,12},{1,17},{... | collective-permute-start | bytes 786440 | tf_op jit(solution)/shard_map/ppermute | solution.py:619
  109.8 26.9 %collective-permute-start.50 = (f32[64,512]{1,0:T(8,128)S(1)}, f32[64,512]{1,0:T(8,128)S(1)}, u32[]{:S(2)}, u32[]{:S(2)}) collective-permute-start(f32[64,512]{1,0:T(8,128)S(1)} %get-tuple-element.263), channel_id=1, source_target_pairs={{0,8},{4,12},{8,0},{12,4},{16,24},{20,28},{24,16},{28,20},{1,9},{5... | collective-permute-start | bytes 393224 | tf_op jit(solution)/shard_map/ppermute | solution.py:619
  128.1 10.7 %collective-permute-start.57 = (f32[128,512]{1,0:T(8,128)S(1)}, f32[128,512]{1,0:T(8,128)S(1)}, u32[]{:S(2)}, u32[]{:S(2)}) collective-permute-start(f32[128,512]{1,0:T(8,128)S(1)} %add.10.refs_2_.refs_0_), channel_id=1, source_target_pairs={{0,4},{4,0},{8,12},{12,8},{16,20},{20,16},{24,28},{28,24},{1,5},{5... | collective-permute-start | bytes 786440 | tf_op jit(solution)/shard_map/ppermute | solution.py:619
  143.5 27.9 %collective-permute-start.67 = (f32[256,512]{1,0:T(8,128)S(1)}, f32[256,512]{1,0:T(8,128)S(1)}, u32[]{:S(2)}, u32[]{:S(2)}) collective-permute-start(f32[256,512]{1,0:T(8,128)S(1)} %join.4.refs_2_.refs_0_), channel_id=1, source_target_pairs={{0,8},{4,12},{8,0},{12,4},{16,24},{20,28},{24,16},{28,20},{1,9},{5... | collective-permute-start | bytes 1572872 | tf_op jit(solution)/shard_map/ppermute | solution.py:619
  143.8 28.5 %collective-permute-start.66 = (f32[256,512]{1,0:T(8,128)S(1)}, f32[256,512]{1,0:T(8,128)S(1)}, u32[]{:S(2)}, u32[]{:S(2)}) collective-permute-start(f32[256,512]{1,0:T(8,128)S(1)} %join.5.refs_8_.refs_0_), channel_id=1, source_target_pairs={{0,4},{4,0},{8,12},{12,8},{16,20},{20,16},{24,28},{28,24},{1,5},{5... | collective-permute-start | bytes 1572872 | tf_op jit(solution)/shard_map/ppermute | solution.py:619
  144.0 15.5 %collective-permute-start.58 = (f32[64,512]{1,0:T(8,128)S(1)}, f32[64,512]{1,0:T(8,128)S(1)}, u32[]{:S(2)}, u32[]{:S(2)}) collective-permute-start(f32[64,512]{1,0:T(8,128)S(1)} %get-tuple-element.268.refs_0_), channel_id=1, source_target_pairs={{0,16},{4,20},{8,24},{12,28},{16,0},{20,4},{24,8},{28,12},{1,17},{... | collective-permute-start | bytes 393224 | tf_op jit(solution)/shard_map/ppermute | solution.py:619
  147.3 14.6 %collective-permute-start.61 = (f32[64,512]{1,0:T(8,128)S(1)}, f32[64,512]{1,0:T(8,128)S(1)}, u32[]{:S(2)}, u32[]{:S(2)}) collective-permute-start(f32[64,512]{1,0:T(8,128)S(1)} %add.13.refs_6_.refs_0_), channel_id=1, source_target_pairs={{0,16},{4,20},{8,24},{12,28},{16,0},{20,4},{24,8},{28,12},{1,17},{... | collective-permute-start | bytes 393224 | tf_op jit(solution)/shard_map/ppermute | solution.py:619
  147.3 12.1 %collective-permute-start.59 = (f32[8,512]{1,0:T(8,128)S(1)}, f32[8,512]{1,0:T(8,128)S(1)}, u32[]{:S(2)}, u32[]{:S(2)}) collective-permute-start(f32[8,512]{1,0:T(8,128)S(1)} %get-tuple-element.264.refs_2_.refs_1_), channel_id=1, source_target_pairs={{0,16},{4,20},{8,24},{12,28},{16,0},{20,4},{24,8},{28,12},{1,17},{... | collective-permute-start | bytes 49160 | tf_op jit(solution)/shard_map/ppermute | solution.py:619
  (47 other events, 243.0 us)
